TPU v7x, 256 devices: a whole 4x4x8 slice. The times are simulated.
256 devices in a mesh: snap: 4 (over x), cell: 64 (over z, y, core).
Axes of the slice: x: 4, y: 4, z: 8, core: 2. Of those that a mesh axis runs over, the one named last changes fastest.
Arguments:
- start_states: float32 [1024, 131072], P('snap', 'cell'), may hold values from -6 to 6
- sources: bfloat16 [2, 1024, 131072], P(None, 'snap', 'cell'), may hold values from -40 to 40
- blocks: bfloat16 [2048, 64, 448], P('cell'), may hold values from -0.25 to 0.25
- columns: int32 [2048, 7], P('cell'), may hold values from 0 to 2047, as said below
- leaf_sketch: float32 [200, 512], replicated, may hold values from -1 to 2
- merge_sketch: float32 [2, 200, 400], replicated, may hold values from -1 to 2
Outputs:
- projected: float32 [1024, 131072], P('snap', 'cell')
Inputs may be any that keep to these rules, and one draw needn't show every extreme that they name: columns[b, 0] = b, and every entry lies within 4 of b.
All inputs are finite; a program needn't handle non-finite values.
Results may differ from a plain program's by a relative error of at most 0.0014.
Values may be sent and summed in bfloat16 or wider, within the bound.
A program may use at most 128 MiB of HBM per device.

v0:
```python
import jax
import jax.numpy as jnp
from jax import lax
from jax.sharding import PartitionSpec as P

HB = 4
STEPS = 2


def with_halo(block, sides, width):
    for axis, dim in sides:
        count = lax.axis_size(axis)
        forward = [(i, i + 1) for i in range(count - 1)]
        backward = [(target, source) for source, target in forward]
        low = lax.ppermute(
            lax.slice_in_dim(block, block.shape[dim] - width, None, axis=dim), axis, forward
        )
        high = lax.ppermute(lax.slice_in_dim(block, 0, width, axis=dim), axis, backward)
        block = jnp.concatenate([low, block, high], axis=dim)
    return block


def swapped(value, axis, apart):
    mask = 2**apart
    pairs = [(source, source ^ mask) for source in range(lax.axis_size(axis))]
    return lax.ppermute(value, axis, pairs)


def gram_of(z_rows):
    return jnp.dot(z_rows, z_rows.T, precision=lax.Precision.HIGHEST)


def normalize(z_rows, gram):
    lower = jnp.linalg.cholesky(gram)
    return lax.linalg.triangular_solve(lower, z_rows, left_side=True, lower=True)


def local(start_states, sources, blocks, columns, leaf_sketch, merge_sketch):
    rows, width = start_states.shape
    nblocks = blocks.shape[0]
    block = blocks.shape[1]
    nstored = blocks.shape[2] // block
    rank = leaf_sketch.shape[0]
    first_block = lax.axis_index("cell") * nblocks
    local_cols = (columns - first_block + HB).reshape(-1)
    state = start_states
    snaps = []
    for step in range(STEPS):
        state_bf = state.astype(jnp.bfloat16)
        padded = with_halo(state_bf, (("cell", 1),), HB * block)
        padded = padded.reshape(rows, nblocks + 2 * HB, block)
        picked = jnp.take(padded, local_cols, axis=1).reshape(rows, nblocks, nstored * block)
        result = jnp.einsum("mbk,brk->mbr", picked, blocks, preferred_element_type=jnp.float32)
        state = state - result.reshape(rows, width) + sources[step].astype(jnp.float32)
        snaps.append(state)
    stacked = jnp.concatenate(snaps, axis=0)
    leaf_rows = jnp.dot(leaf_sketch, stacked, precision=lax.Precision.HIGHEST)
    leaf_total = lax.psum(gram_of(leaf_rows), "cell")
    basis = normalize(leaf_rows, leaf_total)
    member = lax.axis_index("snap")
    top_rows = basis
    for level in range(2):
        other = swapped(basis, "snap", level)
        upper = member // (1 << level) % 2
        sketch = merge_sketch[level]
        own_part = jnp.where(upper == 1, sketch[:, rank:], sketch[:, :rank])
        other_part = jnp.where(upper == 1, sketch[:, :rank], sketch[:, rank:])
        merged = jnp.dot(own_part, basis, precision=lax.Precision.HIGHEST) + jnp.dot(
            other_part, other, precision=lax.Precision.HIGHEST
        )
        if level == 0:
            pair_total = lax.psum(gram_of(merged), "cell")
            basis = normalize(merged, pair_total)
        else:
            top_rows = merged
    top_total = lax.psum(gram_of(top_rows), "cell")
    final_basis = normalize(top_rows, top_total)
    coeffs = lax.psum(jnp.dot(state, final_basis.T, precision=lax.Precision.HIGHEST), "cell")
    projected = jnp.dot(coeffs, final_basis, precision=lax.Precision.HIGHEST)
    return projected


def solution(mesh):
    placed = (
        P("snap", "cell"),
        P(None, "snap", "cell"),
        P("cell", None, None),
        P("cell", None),
        P(),
        P(),
    )
    return jax.shard_map(
        local, mesh=mesh, in_specs=placed, out_specs=P("snap", "cell"), check_vma=False
    )
```

profile of v0, /device:TPU:1, one launch (start us, length us, event | category | flops | bytes accessed | tf_op | source)
XLA Modules:
  0.0 1040.1 jit_solution(8449918252533428719)
XLA Ops:
  6.5 3.0 copy.19
  12.3 4.6 collective-permute-start
  24.7 8.4 gather_fusion
  33.0 3.8 broadcast_select_fusion.1
  41.4 3.5 collective-permute-start.2
  48.4 2.9 collective-permute-done.3
  52.7 8.4 gather_fusion.1
  61.1 3.8 broadcast_select_fusion
  67.8 4.5 fusion
  74.8 179.8 %all-reduce.8.cloned.1.call-done = f32[200,200]{0,1:T(8,128)} async-done(((f32[200,200]{0,1:T(8,128)}), f32[200,200]{0,1:T(8,128)}) %all-reduce.8.cloned.1.call-update) | async-done | bytes 160016 | tf_op jit(solution)/shard_map/psum | solution.py:58
  256.5 11.7 %cholesky.182 = f32[128,128]{1,0:T(8,128)S(1)} custom-call(f32[128,128]{1,0:T(8,128)S(1)} %cholesky.292), custom_call_target="Cholesky" | custom-call | tf_op jit(solution)/shard_map/jit(cholesky)/cholesky | solution.py:34
  268.3 9.8 custom-call.15
  278.6 6.6 cholesky.202
  288.0 20.1 %custom-call.16 = f32[2,128,128]{1,2,0:T(8,128)S(1)} custom-call(f32[2,128,128]{2,1,0:T(8,128)S(1)} %pad_maximum_fusion.7), custom_call_target="InvertDiagBlocksLowerTriangular" | custom-call | tf_op jit(solution)/shard_map/triangular_solve/custom-call.0 | solution.py:35
  314.7 34.8 %collective-permute-done.4 = f32[200,2048]{1,0:T(8,128)} collective-permute-done((f32[200,2048]{1,0:T(8,128)}, f32[200,2048]{1,0:T(8,128)}, u32[]{:S(2)}, u32[]{:S(2)}) %collective-permute-start.4) | collective-permute-done | bytes 1638432 | tf_op jit(solution)/shard_map/ppermute | solution.py:26
  349.5 3.0 convolution_add_fusion.1
  354.9 169.5 %all-reduce.10.cloned.1.call-done = f32[200,200]{0,1:T(8,128)} async-done(((f32[200,200]{0,1:T(8,128)}), f32[200,200]{0,1:T(8,128)}) %all-reduce.10.cloned.1.call-update) | async-done | bytes 160016 | tf_op jit(solution)/shard_map/psum | solution.py:72
  526.5 11.7 %cholesky.220 = f32[128,128]{1,0:T(8,128)S(1)} custom-call(f32[128,128]{1,0:T(8,128)S(1)} %cholesky.295), custom_call_target="Cholesky" | custom-call | tf_op jit(solution)/shard_map/jit(cholesky)/cholesky | solution.py:34
  538.2 9.8 custom-call.17
  548.5 6.6 cholesky.240
  557.9 19.9 %custom-call.18 = f32[2,128,128]{1,2,0:T(8,128)S(1)} custom-call(f32[2,128,128]{2,1,0:T(8,128)S(1)} %pad_maximum_fusion.8), custom_call_target="InvertDiagBlocksLowerTriangular" | custom-call | tf_op jit(solution)/shard_map/triangular_solve/custom-call.0 | solution.py:35
  581.2 2.8 collective-permute-start.5
  586.6 33.6 %collective-permute-done.5 = f32[200,2048]{1,0:T(8,128)} collective-permute-done((f32[200,2048]{1,0:T(8,128)S(1)}, f32[200,2048]{1,0:T(8,128)}, u32[]{:S(2)}, u32[]{:S(2)}) %collective-permute-start.5) | collective-permute-done | bytes 1638432 | tf_op jit(solution)/shard_map/ppermute | solution.py:26
  620.2 3.0 convolution_add_fusion
  625.7 169.4 %all-reduce.12.cloned.1.call-done = f32[200,200]{0,1:T(8,128)} async-done(((f32[200,200]{0,1:T(8,128)}), f32[200,200]{0,1:T(8,128)}) %all-reduce.12.cloned.1.call-update) | async-done | bytes 160016 | tf_op jit(solution)/shard_map/psum | solution.py:76
  797.1 11.7 %cholesky.258 = f32[128,128]{1,0:T(8,128)S(1)} custom-call(f32[128,128]{1,0:T(8,128)S(1)} %cholesky.298), custom_call_target="Cholesky" | custom-call | tf_op jit(solution)/shard_map/jit(cholesky)/cholesky | solution.py:34
  808.9 9.8 custom-call.19
  819.1 6.6 cholesky.278
  828.5 20.0 %custom-call.20 = f32[2,128,128]{1,2,0:T(8,128)S(1)} custom-call(f32[2,128,128]{2,1,0:T(8,128)S(1)} %pad_maximum_fusion.9), custom_call_target="InvertDiagBlocksLowerTriangular" | custom-call | tf_op jit(solution)/shard_map/triangular_solve/custom-call.0 | solution.py:35
  851.8 4.2 fusion.5
  856.1 172.7 %all-reduce.14.cloned.1.call-done = f32[256,200]{1,0:T(8,128)} async-done(((f32[256,200]{1,0:T(8,128)}), f32[256,200]{1,0:T(8,128)}) %all-reduce.14.cloned.1.call-update) | async-done | bytes 204816 | tf_op jit(solution)/shard_map/psum | solution.py:78
  1028.8 4.3 fusion.4
  (127 shorter events, 57.8 us)
Async XLA Ops:
  6.5 30.3 %copy-start = (bf16[32,64,448]{2,1,0:T(8,128)(2,1)S(1)}, bf16[32,64,448]{2,1,0:T(8,128)(2,1)}, u32[]{:S(2)}) copy-start(bf16[32,64,448]{2,1,0:T(8,128)(2,1)} %param.13) | copy-start | bytes 5505028
  6.5 248.0 %all-reduce.8.cloned.1.call-start = ((), (), s32[]{:S(2)}) async-start(), calls=%async_computation | async-start | bytes 409600 | tf_op jit(solution)/shard_map/psum | solution.py:58
  9.6 9.3 copy-start.15
  11.3 1.0 copy-start.6
  12.3 10.9 %collective-permute-start = (bf16[256,256]{0,1:T(8,128)(2,1)S(1)}, bf16[256,256]{0,1:T(8,128)(2,1)S(1)}, u32[]{:S(2)}, u32[]{:S(2)}) collective-permute-start(bf16[256,256]{0,1:T(8,128)(2,1)S(1)} %get-tuple-element.46), channel_id=1, source_target_pairs={{0,1},{1,2},{2,3},{3,4},{4,5},{5,6},{6,7},{7,8},{8,9},{9,10},{10,1... | collective-permute-start | bytes 393224 | tf_op jit(solution)/shard_map/ppermute | solution.py:15
  16.9 6.4 collective-permute-start.1
  36.9 1.6 copy-start.5
  36.9 1.8 copy-start.12
  38.7 8.3 copy-start.11
  40.4 1.0 copy-start.9
  41.4 7.0 collective-permute-start.2
  44.9 6.4 collective-permute-start.3
  64.9 1.6 copy-start.4
  64.9 1.8 copy-start.10
  66.7 1.0 copy-start.14
  67.7 4.5 copy-start.2
  74.4 450.0 %all-reduce.10.cloned.1.call-start = ((), (), s32[]{:S(2)}) async-start(), calls=%async_computation.1 | async-start | bytes 409600 | tf_op jit(solution)/shard_map/psum | solution.py:72
  310.6 2.5 copy-start.13
  311.9 37.6 %collective-permute-start.4 = (f32[200,2048]{1,0:T(8,128)}, f32[200,2048]{1,0:T(8,128)}, u32[]{:S(2)}, u32[]{:S(2)}) collective-permute-start(f32[200,2048]{1,0:T(8,128)} %pad_maximum_fusion), channel_id=1, source_target_pairs={{0,64},{64,0},{128,192},{192,128},{1,65},{65,1},{129,193},{193,129... | collective-permute-start | bytes 4915208 | tf_op jit(solution)/shard_map/ppermute | solution.py:26
  354.7 440.4 %all-reduce.12.cloned.1.call-start = ((), (), s32[]{:S(2)}) async-start(), calls=%async_computation.2 | async-start | bytes 409600 | tf_op jit(solution)/shard_map/psum | solution.py:76
  580.3 0.8 copy-start.7
  581.2 39.0 %collective-permute-start.5 = (f32[200,2048]{1,0:T(8,128)S(1)}, f32[200,2048]{1,0:T(8,128)}, u32[]{:S(2)}, u32[]{:S(2)}) collective-permute-start(f32[200,2048]{1,0:T(8,128)S(1)} %pad_maximum_fusion.1), channel_id=1, source_target_pairs={{0,128},{64,192},{128,0},{192,64},{1,129},{65,193},{129,1},{193,65... | collective-permute-start | bytes 4915208 | tf_op jit(solution)/shard_map/ppermute | solution.py:26
  625.4 403.4 %all-reduce.14.cloned.1.call-start = ((), (), s32[]{:S(2)}) async-start(), calls=%async_computation.3 | async-start | bytes 524288 | tf_op jit(solution)/shard_map/psum | solution.py:78
  849.6 2.2 copy-start.3
  851.0 0.8 copy-start.8
  856.1 177.0 %copy-start.1 = (bf16[32,64,448]{2,1,0:T(8,128)(2,1)S(1)}, bf16[32,64,448]{2,1,0:T(8,128)(2,1)}, u32[]{:S(2)}) copy-start(bf16[32,64,448]{2,1,0:T(8,128)(2,1)} %param.13) | copy-start | bytes 5505028
Sparse Core Ops, SparseCore 0:
  74.6 179.9 all-reduce.7
  354.8 169.5 all-reduce.9
  625.5 169.5 all-reduce.11
  856.2 172.5 all-reduce.13
where the time goes:
time: 1050 us; the launch traced here: 1040 us
  waiting for transfers between devices  763 us (73%)
  other arithmetic  167 us (16%)
  matrix products  41 us (4%)
  local copies, waits for them, and re-layouts  33.8 us (3%)
  between operations  18.1 us (2%)
  starting transfers between devices  17 us (2%)
    psum x1, waiting for transfers between devices, local(): leaf_total = lax.psum(gram_of(leaf_rows), 'cell')  180 us
    psum x1, waiting for transfers between devices, local(): lax.psum(jnp.dot(state, final_basis.T, precision=lax.Precision.HIGHEST),...  173 us
    psum x1, waiting for transfers between devices, local(): pair_total = lax.psum(gram_of(merged), 'cell')  170 us
    psum x1, waiting for transfers between devices, local(): top_total = lax.psum(gram_of(top_rows), 'cell')  169 us
    another operation x21, other arithmetic, normalize(): lower = jnp.linalg.cholesky(gram)  88.6 us
    ppermute x2, waiting for transfers between devices, swapped(): return lax.ppermute(value, axis, pairs)  68.4 us
    another operation x16, other arithmetic, normalize(): lax.linalg.triangular_solve(lower, z_rows, left_side=True, lower=True)  61.8 us
  transfers between devices with their start and end apart: 10, of which 8 were waited for; matrix products, arithmetic and copies ran while one was open for 1% of the time, Pallas kernels for 0%

commit v1 on v0

v1 whole, which is shorter than its diff:
```python
import jax
import jax.numpy as jnp
from jax import lax
from jax.experimental import pallas as pl
from jax.experimental.pallas import tpu as pltpu
from jax.sharding import PartitionSpec as P

HB = 4
NZ = 8
NW = 8
NX = 4
NB = 40
MESH = pl.DeviceIdType.MESH
F32 = jnp.float32
BF16 = jnp.bfloat16


def mm(a, b):
    return jnp.dot(a, b, precision=lax.Precision.HIGHEST, preferred_element_type=F32)


def mm_nt(a, b):
    return lax.dot_general(
        a, b, (((1,), (1,)), ((), ())), precision=lax.Precision.HIGHEST, preferred_element_type=F32
    )


def mm_tn(a, b):
    return lax.dot_general(
        a, b, (((0,), (0,)), ((), ())), precision=lax.Precision.HIGHEST, preferred_element_type=F32
    )


def snap_kernel(
    x0_ref, src_ref, blk_ref, cols_ref, sk_ref,
    x2_ref, y_ref, g_ref,
    x1_ref, dup_a, dup_b, out_h, in_h, send_sem, recv_sem,
):
    x = lax.axis_index("snap")
    c = lax.axis_index("cell")
    n = 64
    left, right = lax.rem(c + n - 1, n), lax.rem(c + 1, n)
    barrier = pltpu.get_barrier_semaphore()
    for peer in (left, right):
        pl.semaphore_signal(barrier, inc=1, device_id=(x, peer), device_id_type=MESH)
    rows = x0_ref.shape[0]
    npair = x0_ref.shape[1] // 128
    low = lax.broadcasted_iota(jnp.int32, (rows, 128), 1) < 64

    def spread(tile, dup, p):
        turned = pltpu.roll(tile, 64, axis=1)
        dup[2 * p] = jnp.where(low, tile, turned).astype(BF16)
        dup[2 * p + 1] = jnp.where(low, turned, tile).astype(BF16)

    def lanes(p):
        return pl.ds(pl.multiple_of(p * 128, 128), 128)

    def copies(step):
        return [
            pltpu.make_async_remote_copy(
                src_ref=out_h.at[step, pl.ds(2 * side, 2)],
                dst_ref=in_h.at[step, pl.ds(2 - 2 * side, 2)],
                send_sem=send_sem.at[step, side],
                recv_sem=recv_sem.at[step, side],
                device_id=(x, peer),
                device_id_type=MESH,
            )
            for side, peer in ((0, left), (1, right))
        ]

    def apply(dup, xin, xout, s, p, then):
        halves = []
        for b2 in range(2):
            b = 2 * p + b2
            parts = []
            for jj in range(3):
                ca = cols_ref[b, 2 * jj]
                cb = cols_ref[b, 2 * jj + 1]
                parts.append(jnp.where(low, dup[ca], dup[cb]))
            parts.append(dup[cols_ref[b, 6]][:, :64])
            picked = jnp.concatenate(parts, axis=1)
            halves.append(
                lax.dot_general(
                    picked, blk_ref[b], (((1,), (1,)), ((), ())), preferred_element_type=F32
                )
            )
        res = jnp.concatenate(halves, axis=1)
        new = xin[:, lanes(p)] - res + src_ref[s, :, lanes(p)].astype(F32)
        xout[:, lanes(p)] = new
        if then is not None:
            spread(new, then, p + 2)
        return new

    for e in range(2):
        out_h[0, e] = x0_ref[:, e * 128 : (e + 1) * 128].astype(BF16)
        q = npair - 2 + e
        out_h[0, 2 + e] = x0_ref[:, q * 128 : (q + 1) * 128].astype(BF16)
    pl.semaphore_wait(barrier, 2)
    first = copies(0)
    for cp in first:
        cp.start()

    @pl.loop(0, npair)
    def _(p):
        spread(x0_ref[:, lanes(p)], dup_a, p + 2)

    @pl.loop(2, npair - 2)
    def _(p):
        apply(dup_a, x0_ref, x1_ref, 0, p, dup_b)

    def arrive(step, dup):
        for e in range(2):
            spread(in_h[step, e].astype(F32), dup, e)
            spread(in_h[step, 2 + e].astype(F32), dup, npair + 2 + e)

    for cp in first:
        cp.wait()
    arrive(0, dup_a)
    for e, p in enumerate((0, 1, npair - 2, npair - 1)):
        out_h[1, e] = apply(dup_a, x0_ref, x1_ref, 0, p, dup_b).astype(BF16)
    second = copies(1)
    for cp in second:
        cp.start()

    @pl.loop(2, npair - 2)
    def _(p):
        apply(dup_b, x1_ref, x2_ref, 1, p, None)

    for cp in second:
        cp.wait()
    arrive(1, dup_b)
    for p in (0, 1, npair - 2, npair - 1):
        apply(dup_b, x1_ref, x2_ref, 1, p, None)

    for q in range(4):
        cut = slice(q * 512, (q + 1) * 512)
        y_ref[q] = mm(sk_ref[:, :rows], x1_ref[:, cut]) + mm(sk_ref[:, rows:], x2_ref[:, cut])
        y = y_ref[q]
        g = mm_nt(y, y)
        if q == 0:
            g_ref[...] = g
        else:
            g_ref[...] += g


def snapshots(start_states, sources, blocks, cols, leaf_sketch):
    rows, width = start_states.shape
    rank = leaf_sketch.shape[0]
    nblk = width // 64
    vmem = pl.BlockSpec(memory_space=pltpu.VMEM)
    return pl.pallas_call(
        snap_kernel,
        name="snapshots",
        out_shape=(
            jax.ShapeDtypeStruct((rows, width), F32),
            jax.ShapeDtypeStruct((4, rank, width // 4), F32),
            jax.ShapeDtypeStruct((rank, rank), F32),
        ),
        in_specs=[vmem, vmem, vmem, pl.BlockSpec(memory_space=pltpu.SMEM), vmem],
        out_specs=(vmem, vmem, vmem),
        scratch_shapes=[
            pltpu.VMEM((rows, width), F32),
            pltpu.VMEM((nblk + 2 * HB, rows, 128), BF16),
            pltpu.VMEM((nblk + 2 * HB, rows, 128), BF16),
            pltpu.VMEM((2, 4, rows, 128), BF16),
            pltpu.VMEM((2, 4, rows, 128), BF16),
            pltpu.SemaphoreType.DMA((2, 2)),
            pltpu.SemaphoreType.DMA((2, 2)),
        ],
        compiler_params=pltpu.CompilerParams(
            collective_id=0, has_side_effects=True, vmem_limit_bytes=48 * 2**20
        ),
    )(start_states, sources, blocks, cols, leaf_sketch)


def eliminate(tiles):
    nt = len(tiles[0])
    sub = lax.broadcasted_iota(jnp.int32, (8, 128), 0)
    for t in range(nt):
        cols = [
            [
                [jnp.broadcast_to(r[u][:, 8 * t + j : 8 * t + j + 1], (8, 128)) for j in range(8)]
                for u in range(t, nt)
            ]
            for r in tiles
        ]
        for j in range(8):
            for r, cl in zip(tiles, cols):
                pivot = jnp.broadcast_to(cl[0][j][j : j + 1], (8, 128))
                inv = lax.rsqrt(pivot)
                row = jnp.broadcast_to(r[t][j : j + 1], (8, 128)) * inv
                heads = [jnp.broadcast_to(cl[0][j][m : m + 1], (8, 128)) * inv for m in range(j + 1, 8)]
                for u in range(t, nt):
                    lcol = cl[u - t][j] * inv
                    if u == t:
                        lcol = jnp.where(sub > j, lcol, 0.0)
                        r[u] = jnp.where(sub == j, row, r[u] - lcol * row)
                    else:
                        r[u] = r[u] - lcol * row
                    for m in range(j + 1, 8):
                        cl[u - t][m] = cl[u - t][m] - lcol * heads[m - j - 1]
    return tiles


def chol_inv(a_ref, t_ref, batch):
    n = a_ref.shape[1]
    steps = n // NB
    r_io = lax.broadcasted_iota(jnp.int32, (n, 256), 0)
    c_io = lax.broadcasted_iota(jnp.int32, (n, 256), 1)
    eye = jnp.where(r_io == c_io, 1.0, 0.0).astype(F32)
    for b in range(batch):
        t_ref[b] = eye
    lane = lax.broadcasted_iota(jnp.int32, (NB, 128), 1)
    srow = lax.broadcasted_iota(jnp.int32, (NB, 128), 0)
    lane2 = lax.broadcasted_iota(jnp.int32, (NB, 256), 1)

    @pl.loop(0, steps)
    def _(k):
        rows = pl.ds(pl.multiple_of(k * NB, 8), NB)
        tiles = []
        for b in range(batch):
            blk = pltpu.roll(a_ref[b, rows, :], lax.rem(256 - k * NB, 256), axis=1)[:, :128]
            blk = jnp.where(lane < NB, blk, jnp.where(lane == 64 + srow, 1.0, 0.0))
            tiles.append([blk[8 * t : 8 * t + 8] for t in range(NB // 8)])
        tiles = eliminate(tiles)
        for b in range(batch):
            tk = pltpu.roll(jnp.concatenate(tiles[b], axis=0), 64, axis=1)[:, :NB]
            wa = mm(tk, a_ref[b, rows, :])
            wt = mm(tk, t_ref[b, rows, :])
            wm = jnp.where((lane2 >= (k + 1) * NB) & (lane2 < n), wa, 0.0)
            lt = wm.T[:n]
            a_ref[b] = a_ref[b] - mm(lt, wa)
            t_ref[b] = t_ref[b] - mm(lt, wt)
            t_ref[b, rows, :] = wt


def exchange(src_of, dst, count, me, device_of, send_sem, recv_sem):
    sends, waits = [], []
    for d in range(1, count):
        peer = lax.rem(me + d, count)
        cp = pltpu.make_async_remote_copy(
            src_ref=src_of(peer), dst_ref=dst.at[me], send_sem=send_sem.at[d], recv_sem=recv_sem.at[me],
            device_id=device_of(peer), device_id_type=MESH,
        )
        cp.start()
        sends.append(cp)
        origin = lax.rem(me + count - d, count)
        waits.append(
            pltpu.make_async_remote_copy(
                src_ref=src_of(peer), dst_ref=dst.at[origin], send_sem=send_sem.at[d], recv_sem=recv_sem.at[origin],
                device_id=device_of(peer), device_id_type=MESH,
            )
        )
    return sends, waits


def finish(pair):
    sends, waits = pair
    for w in waits:
        w.wait_recv()
    for s in sends:
        s.wait_send()


def add_up(ref, count):
    total = ref[0]
    for i in range(1, count):
        total = total + ref[i]
    return total


class Where:
    def __init__(self):
        self.x = lax.axis_index("snap")
        c = lax.axis_index("cell")
        self.z, self.w = c // NW, lax.rem(c, NW)

    def along_z(self, peer):
        return (self.x, peer * NW + self.w)

    def along_w(self, peer):
        return (self.x, self.z * NW + peer)

    def along_x(self, peer):
        return (peer, self.z * NW + self.w)


def reduce_all(at, pk, size, bufs, mode, between=None):
    r1, r2, rx, out, ss, rs = bufs

    def piece(peer):
        return pk.at[pl.ds(pl.multiple_of(peer * size, 8), size)]

    r1[at.z] = pk[pl.ds(pl.multiple_of(at.z * size, 8), size), :]
    finish(exchange(piece, r1, NZ, at.z, at.along_z, ss.at[0], rs.at[0]))
    r2[at.w] = add_up(r1, NZ)
    finish(exchange(lambda _: r2.at[at.w], r2, NW, at.w, at.along_w, ss.at[1], rs.at[1]))
    total = add_up(r2, NW)
    if mode == "cell":
        out[at.z] = total
    else:
        rx[at.x] = total
        finish(exchange(lambda _: rx.at[at.x], rx, NX, at.x, at.along_x, ss.at[2], rs.at[2]))
        out[at.z] = add_up(rx, NX) if mode == "sum" else rx[...]
    if between is not None:
        between()
    finish(exchange(lambda _: out.at[at.z], out, NZ, at.z, at.along_z, ss.at[3], rs.at[3]))


def pack(g, g_ref, pk, base):
    g_ref[:, : g.shape[1]] = g
    pk[base : base + 200, :] = g_ref[:, :128]
    pk[base + 200 : base + 272, :] = g_ref[128:200, 128:]


def unpack(pk, base, a_ref, b):
    a_ref[b, :, :128] = pk[base : base + 200, :]
    a_ref[b, 128:200, 128:] = pk[base + 200 : base + 272, :]
    a_ref[b, :128, 128:] = pk[base + 128 : base + 256, :].T


def merge_kernel(
    y_ref, g_ref, x2_ref, ms_ref,
    zf_ref, co_ref,
    yq, m_ref, gs, a4, t4, flat,
    pk1, l1, l2, lx, lo, pk2, p1, p2, px, po, pk3, c1, c2, co,
    s1, q1, s2, q2, s3, q3, sb, qb,
):
    at = Where()
    n = 200
    barrier = pltpu.get_barrier_semaphore()
    for d in range(1, NZ):
        pl.semaphore_signal(barrier, inc=1, device_id=at.along_z(lax.rem(at.z + d, NZ)), device_id_type=MESH)
        pl.semaphore_signal(barrier, inc=1, device_id=at.along_w(lax.rem(at.w + d, NW)), device_id_type=MESH)
    for d in range(1, NX):
        pl.semaphore_signal(barrier, inc=1, device_id=at.along_x(lax.rem(at.x + d, NX)), device_id_type=MESH)
    gs[...] = jnp.zeros_like(gs)
    pk1[...] = jnp.zeros_like(pk1)
    pk2[...] = jnp.zeros_like(pk2)
    pk3[...] = jnp.zeros_like(pk3)
    pack(g_ref[...], gs, pk1, 0)
    pl.semaphore_wait(barrier, 2 * (NZ - 1) + NX - 1)

    bulk = []

    def send_y():
        bulk.append(exchange(lambda peer: y_ref.at[peer], yq, NX, at.x, at.along_x, sb.at[0], qb.at[0]))

    reduce_all(at, pk1, 40, (l1, l2, lx, lo, s1, q1), "gather", between=send_y)
    yq[at.x] = y_ref[at.x]
    for g in range(NX):
        for o in range(NZ):
            flat[o * 40 : (o + 1) * 40, :] = lo[o, g]
        unpack(flat, 0, a4, g)
    chol_inv(a4, t4, NX)
    coef = [mm(ms_ref[0, :, n * (g % 2) : n * (g % 2) + n], t4[g][:, :n]) for g in range(NX)]
    finish(bulk[0])

    for p in range(2):
        m_ref[p] = mm(coef[2 * p], yq[2 * p]) + mm(coef[2 * p + 1], yq[2 * p + 1])
        pack(mm_nt(m_ref[p], m_ref[p]), gs, pk2, 272 * p)
    reduce_all(at, pk2, 72, (p1, p2, px, po, s2, q2), "sum")
    for o in range(NZ):
        flat[o * 72 : (o + 1) * 72, :] = po[o]
    for p in range(2):
        unpack(flat, 272 * p, a4, p)
    chol_inv(a4, t4, 2)
    z = mm(mm(ms_ref[1, :, :n], t4[0][:, :n]), m_ref[0]) + mm(mm(ms_ref[1, :, n:], t4[1][:, :n]), m_ref[1])

    zf_ref[at.x] = z
    finish(exchange(lambda _: zf_ref.at[at.x], zf_ref, NX, at.x, at.along_x, sb.at[1], qb.at[1]))
    gram = mm_nt(zf_ref[0], zf_ref[0])
    raw = mm_nt(x2_ref[:, :512], zf_ref[0])
    for q in range(1, NX):
        gram = gram + mm_nt(zf_ref[q], zf_ref[q])
        raw = raw + mm_nt(x2_ref[:, q * 512 : (q + 1) * 512], zf_ref[q])
    pack(gram, gs, pk3, 512)
    pk3[0:256, :] = raw[:, :128]
    pk3[256:512, :72] = raw[:, 128:]
    reduce_all(at, pk3, 104, (c1, c2, None, co, s3, q3), "cell")
    for o in range(NZ):
        flat[o * 104 : (o + 1) * 104, :] = co[o]
    unpack(flat, 512, a4, 0)
    chol_inv(a4, t4, 1)
    t = t4[0][:, :n]
    first = mm_nt(flat[0:256, :], t[:, :128]) + mm_nt(flat[256:512, :][:, :72], t[:, 128:])
    co_ref[...] = mm(first, t)


def merged(y, g, x2, merge_sketch):
    rank = y.shape[1]
    part = y.shape[2]
    rows = x2.shape[0]
    vmem = pl.BlockSpec(memory_space=pltpu.VMEM)
    dma = pltpu.SemaphoreType.DMA

    def buf(*shape):
        return pltpu.VMEM(shape, F32)

    return pl.pallas_call(
        merge_kernel,
        name="merge",
        out_shape=(
            jax.ShapeDtypeStruct((NX, rank, part), F32),
            jax.ShapeDtypeStruct((rows, rank), F32),
        ),
        in_specs=[vmem] * 4,
        out_specs=(vmem, vmem),
        scratch_shapes=[
            buf(NX, rank, part), buf(2, rank, part), buf(rank, 256), buf(NX, rank, 256), buf(NX, rank, 256),
            buf(832, 128),
            buf(320, 128), buf(NZ, 40, 128), buf(NW, 40, 128), buf(NX, 40, 128), buf(NZ, NX, 40, 128),
            buf(576, 128), buf(NZ, 72, 128), buf(NW, 72, 128), buf(NX, 72, 128), buf(NZ, 72, 128),
            buf(832, 128), buf(NZ, 104, 128), buf(NW, 104, 128), buf(NZ, 104, 128),
            dma((4, 8)), dma((4, 8)), dma((4, 8)), dma((4, 8)), dma((4, 8)), dma((4, 8)), dma((2, 4)), dma((2, 4)),
        ],
        compiler_params=pltpu.CompilerParams(
            collective_id=1, has_side_effects=True, vmem_limit_bytes=48 * 2**20
        ),
    )(y, g, x2, merge_sketch)


def project_kernel(co_ref, z_ref, o_ref):
    o_ref[...] = mm(co_ref[...], z_ref[0])


def project(coeffs, z):
    rows, rank = coeffs.shape
    parts, _, part = z.shape
    return pl.pallas_call(
        project_kernel,
        name="project",
        grid=(parts,),
        out_shape=jax.ShapeDtypeStruct((rows, parts * part), F32),
        in_specs=[
            pl.BlockSpec((rows, rank), lambda q: (0, 0)),
            pl.BlockSpec((1, rank, part), lambda q: (q, 0, 0)),
        ],
        out_specs=pl.BlockSpec((rows, part), lambda q: (0, q)),
        compiler_params=pltpu.CompilerParams(vmem_limit_bytes=32 * 2**20),
    )(coeffs, z)


def local(start_states, sources, blocks, columns, leaf_sketch, merge_sketch):
    cols = columns - lax.axis_index("cell") * blocks.shape[0] + HB
    x2, y, g = snapshots(start_states, sources, blocks, cols, leaf_sketch)
    z, coeffs = merged(y, g, x2, merge_sketch)
    return project(coeffs, z)


def solution(mesh):
    placed = (
        P("snap", "cell"),
        P(None, "snap", "cell"),
        P("cell", None, None),
        P("cell", None),
        P(),
        P(),
    )
    return jax.shard_map(
        local, mesh=mesh, in_specs=placed, out_specs=P("snap", "cell"), check_vma=False
    )
```

time: 1050 us -> 205 us (0.20)
  waiting for transfers between devices: 763 us -> 0 us
  Pallas kernels: 0 us -> 202 us
  other arithmetic: 167 us -> 0.01 us
  matrix products: 41 us -> 0 us
  local copies, waits for them, and re-layouts: 33.8 us -> 3.09 us
  between operations: 18.1 us -> 0.03 us
  starting transfers between devices: 17 us -> 0 us
    psum x4 -> x0, waiting for transfers between devices: 691 us -> none  [the longest x1 180 us: local(): leaf_total = lax.psum(gram_of(leaf_rows), 'cell')]
    pallas_call x0 -> x3, Pallas kernels: none -> 202 us  [the longest x1 172 us: merged(): pl.pallas_call(merge_kernel, name='merge', out_shape=(jax.ShapeDtypeStruc...]
    another operation x37 -> x0, other arithmetic: 150 us -> none  [the longest x21 88.6 us: normalize(): lower = jnp.linalg.cholesky(gram)]
    ppermute x6 -> x0, waiting for transfers between devices: 71.4 us -> none  [the longest x2 68.4 us: swapped(): return lax.ppermute(value, axis, pairs)]
    dot_general x12 -> x0, matrix products: 32.4 us -> none  [the longest x3 6.52 us: gram_of(): return jnp.dot(z_rows, z_rows.T, precision=lax.Precision.HIGHEST)]
    gather x2 -> x0, local copies, waits for them, and re-layouts: 16.7 us -> none  [local(): jnp.take(padded, local_cols, axis=1).reshape(rows, nblocks, nstored * block)]
    ppermute x6 -> x0, starting transfers between devices: 16.1 us -> none  [the longest x2 8.11 us: with_halo(): lax.ppermute(lax.slice_in_dim(block, block.shape[dim] - width, None, axis...]
  transfers between devices with their start and end apart: 10 -> 0, of which waited for: 8 -> 0; matrix products, arithmetic and copies ran while one was open for 1% -> 0% of each run, Pallas kernels for 0% -> 0%
where the time goes in v1:
time: 205 us
  Pallas kernels  202 us (99%)
  local copies, waits for them, and re-layouts  3.09 us (2%)
    pallas_call x1, Pallas kernels, merged(): pl.pallas_call(merge_kernel, name='merge', out_shape=(jax.ShapeDtypeStruc...  172 us
    pallas_call x1, Pallas kernels, snapshots(): pl.pallas_call(snap_kernel, name='snapshots', out_shape=(jax.ShapeDtypeSt...  26.1 us

profile of v1, /device:TPU:1, one launch (start us, length us, event | category | flops | bytes accessed | tf_op | source)
XLA Modules:
  0.0 204.9 jit_solution(2002001083249751964)
XLA Ops:
  0.0 0.8 copy.8
  0.8 0.0 copy-start.2
  0.8 1.0 copy-done.2
  1.8 0.0 copy-start.1
  1.8 26.1 %snapshots.1 = (f32[256,2048]{1,0:T(8,128)S(1)}, f32[4,200,512]{2,1,0:T(8,128)S(1)}, f32[200,200]{1,0:T(8,128)S(1)}) custom-call(f32[256,2048]{1,0:T(8,128)} %x0_ref.1, bf16[2,256,2048]{2,1,0:T(8,128)(2,1)} %src_ref.1, bf16[32,64,448]{2,1,0:T(8,128)(2,1)} %blk_ref.1, s32[32,7]{1,0:T(8,128)S(1)} %subtract_add_fusion.cols_ref, f32[200,512]{1,0:T(8,128)S(1)} %copy-done.2), custom_call_target="tpu_custom_call" | custom-call | tf_op jit(solution)/shard_map/snapshots/pallas_call | solution.py:151
  27.9 0.0 copy-start
  27.9 1.3 copy-done
  29.2 0.0 copy-done.1
  29.2 172.3 %merge.1 = (f32[4,200,512]{2,1,0:T(8,128)S(1)}, f32[256,200]{1,0:T(8,128)S(1)}) custom-call(f32[4,200,512]{2,1,0:T(8,128)S(1)} %get-tuple-element.10.y_ref, f32[200,200]{1,0:T(8,128)S(1)} %get-tuple-element.11.g_ref, f32[256,2048]{1,0:T(8,128)} %copy-done, f32[2,200,400]{2,1,0:T(8,128)S(1)} %copy-done.1), custom_call_target="tpu_custom_call" | custom-call | tf_op jit(solution)/shard_map/merge/pallas_call | solution.py:400
  201.5 3.4 %project.1 = f32[256,2048]{1,0:T(8,128)} custom-call(f32[256,200]{1,0:T(8,128)S(1)} %get-tuple-element.13.co_ref, f32[4,200,512]{2,1,0:T(8,128)S(1)} %get-tuple-element.14.z_ref), custom_call_target="tpu_custom_call" | custom-call | tf_op jit(solution)/shard_map/project/pallas_call | solution.py:430
  (1 shorter events, 0.0 us)
Async XLA Ops:
  0.8 1.0 copy-start.2
  1.8 27.5 %copy-start.1 = (f32[2,200,400]{2,1,0:T(8,128)S(1)}, f32[2,200,400]{2,1,0:T(8,128)}, u32[]{:S(2)}) copy-start(f32[2,200,400]{2,1,0:T(8,128)} %ms_ref.1) | copy-start | bytes 1920004
  27.9 1.3 copy-start

commit v2 on v0

v2 whole, which is shorter than its diff:
```python
import jax
import jax.numpy as jnp
from jax import lax
from jax.experimental import pallas as pl
from jax.experimental.pallas import tpu as pltpu
from jax.sharding import PartitionSpec as P

HB = 4
NZ = 8
NW = 8
NX = 4
NB = 40
MESH = pl.DeviceIdType.MESH
F32 = jnp.float32
BF16 = jnp.bfloat16


def mm(a, b):
    return jnp.dot(a, b, precision=lax.Precision.HIGHEST, preferred_element_type=F32)


def halves(a):
    high = a.astype(BF16)
    return high, (a - high.astype(F32)).astype(BF16)


def mm3(a, b):
    ah, al = halves(a)
    bh, bl = halves(b)
    small = jnp.dot(ah, bl, preferred_element_type=F32) + jnp.dot(al, bh, preferred_element_type=F32)
    return jnp.dot(ah, bh, preferred_element_type=F32) + small


def mm_nt(a, b):
    return lax.dot_general(
        a, b, (((1,), (1,)), ((), ())), precision=lax.Precision.HIGHEST, preferred_element_type=F32
    )


def eliminate(tiles):
    nt = len(tiles[0])
    sub = lax.broadcasted_iota(jnp.int32, (8, 128), 0)
    for t in range(nt):
        cols = [
            [
                [jnp.broadcast_to(r[u][:, 8 * t + j : 8 * t + j + 1], (8, 128)) for j in range(8)]
                for u in range(t, nt)
            ]
            for r in tiles
        ]
        for j in range(8):
            for r, cl in zip(tiles, cols):
                pivot = jnp.broadcast_to(cl[0][j][j : j + 1], (8, 128))
                inv = lax.rsqrt(pivot)
                row = jnp.broadcast_to(r[t][j : j + 1], (8, 128)) * inv
                heads = [jnp.broadcast_to(cl[0][j][m : m + 1], (8, 128)) * inv for m in range(j + 1, 8)]
                for u in range(t, nt):
                    lcol = cl[u - t][j] * inv
                    if u == t:
                        lcol = jnp.where(sub > j, lcol, 0.0)
                        r[u] = jnp.where(sub == j, row, r[u] - lcol * row)
                    else:
                        r[u] = r[u] - lcol * row
                    for m in range(j + 1, 8):
                        cl[u - t][m] = cl[u - t][m] - lcol * heads[m - j - 1]
    return tiles


def chol_inv(a_ref, batch, hooks=()):
    n = a_ref.shape[1]
    lane = lax.broadcasted_iota(jnp.int32, (NB, 128), 1)
    srow = lax.broadcasted_iota(jnp.int32, (NB, 128), 0)
    lane2 = lax.broadcasted_iota(jnp.int32, (NB, 256), 1)
    srow2 = lax.broadcasted_iota(jnp.int32, (NB, 256), 0)
    lane3 = lax.broadcasted_iota(jnp.int32, (n, 256), 1)
    srow3 = lax.broadcasted_iota(jnp.int32, (n, 256), 0)

    def step(k):
        lo = k * NB
        hi = lo + NB
        rows = pl.ds(pl.multiple_of(lo, 8), NB)
        tiles = []
        for b in range(batch):
            blk = pltpu.roll(a_ref[b, rows, :], lax.rem(256 - lo, 256), axis=1)[:, :128]
            blk = jnp.where(lane < NB, blk, jnp.where(lane == 64 + srow, 1.0, 0.0))
            tiles.append([blk[8 * t : 8 * t + 8] for t in range(NB // 8)])
        tiles = eliminate(tiles)
        for b in range(batch):
            tk = pltpu.roll(jnp.concatenate(tiles[b], axis=0), 64, axis=1)[:, :NB]
            own = jnp.where(lane2 - lo == srow2, 1.0, 0.0)
            w = mm(tk, jnp.where((lane2 >= lo) & (lane2 < hi), own, a_ref[b, rows, :]))
            lt = jnp.where((lane2 >= hi) & (lane2 < n), w, 0.0).T[:n]
            rest = jnp.where((lane3 >= lo) & (lane3 < hi) & (srow3 >= hi), 0.0, a_ref[b])
            a_ref[b] = rest - mm(lt, w)
            a_ref[b, rows, :] = jnp.where(lane2 < hi, w, 0.0)

    at = 0
    for stop, call in (*hooks, (n // NB, None)):
        pl.loop(at, stop)(step)
        if call is not None:
            call()
        at = stop


def exchange(src_of, dst, count, me, device_of, send_sem, recv_sem):
    sends, waits = [], []
    for d in range(1, count):
        peer = lax.rem(me + d, count)
        cp = pltpu.make_async_remote_copy(
            src_ref=src_of(peer), dst_ref=dst.at[me], send_sem=send_sem.at[d], recv_sem=recv_sem.at[me],
            device_id=device_of(peer), device_id_type=MESH,
        )
        cp.start()
        sends.append(cp)
        origin = lax.rem(me + count - d, count)
        waits.append(
            pltpu.make_async_remote_copy(
                src_ref=src_of(peer), dst_ref=dst.at[origin], send_sem=send_sem.at[d], recv_sem=recv_sem.at[origin],
                device_id=device_of(peer), device_id_type=MESH,
            )
        )
    return sends, waits


def finish(pair):
    sends, waits = pair
    for w in waits:
        w.wait_recv()
    for s in sends:
        s.wait_send()


def add_up(ref, count):
    total = ref[0]
    for i in range(1, count):
        total = total + ref[i]
    return total


class Where:
    def __init__(self):
        self.x = lax.axis_index("snap")
        self.c = lax.axis_index("cell")
        self.z, self.w = self.c // NW, lax.rem(self.c, NW)

    def along_z(self, peer):
        return (self.x, peer * NW + self.w)

    def along_w(self, peer):
        return (self.x, self.z * NW + peer)

    def along_x(self, peer):
        return (peer, self.z * NW + self.w)


def reduce_steps(at, pk, size, bufs, over_snap):
    r1, r2, rx, out, ss, rs = bufs

    def piece(peer):
        return pk.at[pl.ds(pl.multiple_of(peer * size, 8), size)]

    going = exchange(piece, r1, NW, at.w, at.along_w, ss.at[0], rs.at[0])
    r1[at.w] = pk[pl.ds(pl.multiple_of(at.w * size, 8), size), :]
    yield
    finish(going)
    r2[at.z] = add_up(r1, NW)
    going = exchange(lambda _: r2.at[at.z], r2, NZ, at.z, at.along_z, ss.at[1], rs.at[1])
    yield
    finish(going)
    total = add_up(r2, NZ)
    if over_snap:
        rx[at.x] = total
        going = exchange(lambda _: rx.at[at.x], rx, NX, at.x, at.along_x, ss.at[2], rs.at[2])
        yield
        finish(going)
        total = add_up(rx, NX)
    out[at.w] = total
    going = exchange(lambda _: out.at[at.w], out, NW, at.w, at.along_w, ss.at[3], rs.at[3])
    yield
    finish(going)


def run(steps):
    for _ in steps:
        pass


def pack(g, g_ref, pk, base):
    g_ref[:, : g.shape[1]] = g
    pk[base : base + 200, :] = g_ref[:, :128]
    pk[base + 200 : base + 272, :] = g_ref[128:200, 128:]


def unpack(pk, base, a_ref, b):
    a_ref[b, :, :128] = pk[base : base + 200, :]
    a_ref[b, 128:200, 128:] = pk[base + 200 : base + 272, :]
    a_ref[b, :128, 128:] = pk[base + 128 : base + 256, :].T


def main_kernel(
    x0_hbm, src_hbm, blk_hbm, cols_ref, sk_hbm, ms_hbm,
    zf_ref, co_ref,
    x0_ref, src_ref, blk_ref, sk_ref, ms_ref, x1_ref, x2_ref, y_ref, dup_a, dup_b, out_h, in_h,
    yq, m_ref, gs, u_ref, fac, tx, flat,
    pk1, l1, l2, lo, pk2, p1, p2, px, po, pk3, t1, t2, tw, to, pk4, c1, c2, co,
    in_sem, send_sem, recv_sem, s1, q1, s2, q2, s3, q3, s4, q4, sb, qb,
):
    at = Where()
    x, c = at.x, at.c
    n = 200
    ncell = NZ * NW
    loads = [
        pltpu.make_async_copy(src, dst, in_sem.at[i])
        for i, (src, dst) in enumerate(
            ((x0_hbm, x0_ref), (blk_hbm, blk_ref), (src_hbm, src_ref), (sk_hbm, sk_ref), (ms_hbm, ms_ref))
        )
    ]
    for ld in loads:
        ld.start()
    left, right = lax.rem(c + ncell - 1, ncell), lax.rem(c + 1, ncell)
    barrier = pltpu.get_barrier_semaphore()
    greeted = [(x, left), (x, right)]
    greeted += [at.along_z(lax.rem(at.z + d, NZ)) for d in range(1, NZ)]
    greeted += [at.along_w(lax.rem(at.w + d, NW)) for d in range(1, NW)]
    greeted += [at.along_x(lax.rem(at.x + d, NX)) for d in range(1, NX)]
    for device in greeted:
        pl.semaphore_signal(barrier, inc=1, device_id=device, device_id_type=MESH)

    rows = x0_ref.shape[0]
    npair = x0_ref.shape[1] // 128
    low = lax.broadcasted_iota(jnp.int32, (rows, 128), 1) < 64

    def spread(tile, dup, p):
        turned = pltpu.roll(tile, 64, axis=1)
        dup[2 * p] = jnp.where(low, tile, turned).astype(BF16)
        dup[2 * p + 1] = jnp.where(low, turned, tile).astype(BF16)

    def lanes(p):
        return pl.ds(pl.multiple_of(p * 128, 128), 128)

    def copies(step):
        return [
            pltpu.make_async_remote_copy(
                src_ref=out_h.at[step, pl.ds(2 * side, 2)],
                dst_ref=in_h.at[step, pl.ds(2 - 2 * side, 2)],
                send_sem=send_sem.at[step, side],
                recv_sem=recv_sem.at[step, side],
                device_id=(x, peer),
                device_id_type=MESH,
            )
            for side, peer in ((0, left), (1, right))
        ]

    def apply(dup, xin, xout, s, p, then):
        sides = []
        for b2 in range(2):
            b = 2 * p + b2
            parts = []
            for jj in range(3):
                ca = cols_ref[b, 2 * jj]
                cb = cols_ref[b, 2 * jj + 1]
                parts.append(jnp.where(low, dup[ca], dup[cb]))
            parts.append(dup[cols_ref[b, 6]][:, :64])
            picked = jnp.concatenate(parts, axis=1)
            sides.append(
                lax.dot_general(
                    picked, blk_ref[b], (((1,), (1,)), ((), ())), preferred_element_type=F32
                )
            )
        res = jnp.concatenate(sides, axis=1)
        new = xin[:, lanes(p)] - res + src_ref[s, :, lanes(p)].astype(F32)
        xout[:, lanes(p)] = new
        if then is not None:
            spread(new, then, p + 2)
        return new

    def arrive(step, dup):
        for e in range(2):
            spread(in_h[step, e].astype(F32), dup, e)
            spread(in_h[step, 2 + e].astype(F32), dup, npair + 2 + e)

    loads[0].wait()
    for e in range(2):
        out_h[0, e] = x0_ref[:, e * 128 : (e + 1) * 128].astype(BF16)
        q = npair - 2 + e
        out_h[0, 2 + e] = x0_ref[:, q * 128 : (q + 1) * 128].astype(BF16)
    pl.semaphore_wait(barrier, len(greeted))
    first = copies(0)
    for cp in first:
        cp.start()

    @pl.loop(0, npair)
    def _(p):
        spread(x0_ref[:, lanes(p)], dup_a, p + 2)

    for ld in loads[1:]:
        ld.wait()

    @pl.loop(2, npair - 2)
    def _(p):
        apply(dup_a, x0_ref, x1_ref, 0, p, dup_b)

    for cp in first:
        cp.wait()
    arrive(0, dup_a)
    for e, p in enumerate((0, 1, npair - 2, npair - 1)):
        out_h[1, e] = apply(dup_a, x0_ref, x1_ref, 0, p, dup_b).astype(BF16)
    second = copies(1)
    for cp in second:
        cp.start()

    @pl.loop(2, npair - 2)
    def _(p):
        apply(dup_b, x1_ref, x2_ref, 1, p, None)

    for cp in second:
        cp.wait()
    arrive(1, dup_b)
    for p in (0, 1, npair - 2, npair - 1):
        apply(dup_b, x1_ref, x2_ref, 1, p, None)

    gs[...] = jnp.zeros_like(gs)
    gram = None
    for q in range(NX):
        cut = slice(q * 512, (q + 1) * 512)
        y_ref[q] = mm3(sk_ref[:, :rows], x1_ref[:, cut]) + mm3(sk_ref[:, rows:], x2_ref[:, cut])
        part = mm_nt(y_ref[q], y_ref[q])
        gram = part if gram is None else gram + part

    pk1[272:, :] = jnp.zeros((48, 128), F32)
    pack(gram, gs, pk1, 0)
    steps = reduce_steps(at, pk1, 40, (l1, l2, None, lo, s1, q1), False)
    next(steps)
    bulk = exchange(lambda peer: y_ref.at[peer], yq, NX, x, at.along_x, sb.at[0], qb.at[0])
    yq[x] = y_ref[x]
    run(steps)
    for o in range(NW):
        flat[o * 40 : (o + 1) * 40, :] = lo[o]
    unpack(flat, 0, fac, 0)
    chol_inv(fac.at[pl.ds(0, 1)], 1)
    tx[x, :200] = fac[0, :, :128]
    tx[x, 200:] = fac[0, 128:, 128:]
    share = exchange(lambda _: tx.at[x], tx, NX, x, at.along_x, sb.at[1], qb.at[1])
    pk2[544:, :] = jnp.zeros((32, 128), F32)
    pk3[272:, :] = jnp.zeros((48, 128), F32)
    pk4[256:, :] = jnp.zeros((256, 128), F32)
    finish(share)
    finish(bulk)

    for p in range(2):
        for h in range(2):
            g = 2 * p + h
            sketch = ms_ref[0, :, n * h : n * h + n]
            u_ref[g, :, :128] = mm(sketch, tx[g, :200])
            u_ref[g, :, 128:] = mm(sketch[:, 128:], tx[g, 200:])
        m_ref[p] = mm(u_ref[2 * p, :, :n], yq[2 * p]) + mm(u_ref[2 * p + 1, :, :n], yq[2 * p + 1])
        pack(mm_nt(m_ref[p], m_ref[p]), gs, pk2, 272 * p)
    run(reduce_steps(at, pk2, 72, (p1, p2, px, po, s2, q2), True))
    for o in range(NW):
        flat[o * 72 : (o + 1) * 72, :] = po[o]
    for p in range(2):
        unpack(flat, 272 * p, fac, p)
    chol_inv(fac, 2)
    z = mm(mm(ms_ref[1, :, :n], fac[0][:, :n]), m_ref[0]) + mm(mm(ms_ref[1, :, n:], fac[1][:, :n]), m_ref[1])

    zf_ref[x] = z
    bulk = exchange(lambda _: zf_ref.at[x], zf_ref, NX, x, at.along_x, sb.at[2], qb.at[2])
    pack(mm_nt(z, z), gs, pk3, 0)
    steps = reduce_steps(at, pk3, 40, (t1, t2, tw, to, s3, q3), True)
    for _ in range(4):
        next(steps)
    finish(bulk)
    raw = mm_nt(x2_ref[:, :512], zf_ref[0])
    for q in range(1, NX):
        raw = raw + mm_nt(x2_ref[:, q * 512 : (q + 1) * 512], zf_ref[q])
    pk4[0:256, :] = raw[:, :128]
    pk4[256:512, :72] = raw[:, 128:]
    last = reduce_steps(at, pk4, 64, (c1, c2, None, co, s4, q4), False)
    next(last)
    run(steps)
    for o in range(NW):
        flat[o * 40 : (o + 1) * 40, :] = to[o]
    unpack(flat, 0, fac, 0)
    chol_inv(fac.at[pl.ds(0, 1)], 1, ((3, lambda: next(last)),))
    t = fac[0]
    u_ref[0] = mm(t.T[:n], t)
    run(last)
    for o in range(NW):
        flat[o * 64 : (o + 1) * 64, :] = co[o]
    co_ref[...] = (mm(flat[0:256, :], u_ref[0, :128, :]) + mm(flat[256:512, :][:, :72], u_ref[0, 128:, :]))[:, :n]


def merged_top(start_states, sources, blocks, cols, leaf_sketch, merge_sketch):
    rows, width = start_states.shape
    rank = leaf_sketch.shape[0]
    part = width // NX
    nblk = width // 64
    anywhere = pl.BlockSpec(memory_space=pl.ANY)
    vmem = pl.BlockSpec(memory_space=pltpu.VMEM)
    dma = pltpu.SemaphoreType.DMA

    def buf(*shape, dtype=F32):
        return pltpu.VMEM(shape, dtype)

    return pl.pallas_call(
        main_kernel,
        name="merged_top",
        out_shape=(
            jax.ShapeDtypeStruct((NX, rank, part), F32),
            jax.ShapeDtypeStruct((rows, rank), F32),
        ),
        in_specs=[anywhere] * 3 + [pl.BlockSpec(memory_space=pltpu.SMEM)] + [anywhere] * 2,
        out_specs=(vmem, vmem),
        scratch_shapes=[
            buf(rows, width), buf(*sources.shape, dtype=BF16), buf(*blocks.shape, dtype=BF16),
            buf(*leaf_sketch.shape), buf(*merge_sketch.shape),
            buf(rows, width), buf(rows, width), buf(NX, rank, part),
            buf(nblk + 2 * HB, rows, 128, dtype=BF16), buf(nblk + 2 * HB, rows, 128, dtype=BF16),
            buf(2, 4, rows, 128, dtype=BF16), buf(2, 4, rows, 128, dtype=BF16),
            buf(NX, rank, part), buf(2, rank, part), buf(rank, 256), buf(NX, rank, 256), buf(2, rank, 256),
            buf(NX, 272, 128), buf(576, 128),
            buf(320, 128), buf(NW, 40, 128), buf(NZ, 40, 128), buf(NW, 40, 128),
            buf(576, 128), buf(NW, 72, 128), buf(NZ, 72, 128), buf(NX, 72, 128), buf(NW, 72, 128),
            buf(320, 128), buf(NW, 40, 128), buf(NZ, 40, 128), buf(NX, 40, 128), buf(NW, 40, 128),
            buf(512, 128), buf(NW, 64, 128), buf(NZ, 64, 128), buf(NW, 64, 128),
            dma((5,)), dma((2, 2)), dma((2, 2)),
            dma((4, 8)), dma((4, 8)), dma((4, 8)), dma((4, 8)), dma((4, 8)), dma((4, 8)), dma((4, 8)), dma((4, 8)),
            dma((3, 4)), dma((3, 4)),
        ],
        compiler_params=pltpu.CompilerParams(
            collective_id=0, has_side_effects=True, vmem_limit_bytes=48 * 2**20
        ),
    )(start_states, sources, blocks, cols, leaf_sketch, merge_sketch)


def project_kernel(co_ref, z_ref, o_ref):
    o_ref[...] = mm3(co_ref[...], z_ref[0])


def project(coeffs, z):
    rows, rank = coeffs.shape
    parts, _, part = z.shape
    return pl.pallas_call(
        project_kernel,
        name="project",
        grid=(parts,),
        out_shape=jax.ShapeDtypeStruct((rows, parts * part), F32),
        in_specs=[
            pl.BlockSpec((rows, rank), lambda q: (0, 0)),
            pl.BlockSpec((1, rank, part), lambda q: (q, 0, 0)),
        ],
        out_specs=pl.BlockSpec((rows, part), lambda q: (0, q)),
        compiler_params=pltpu.CompilerParams(vmem_limit_bytes=32 * 2**20),
    )(coeffs, z)


def local(start_states, sources, blocks, columns, leaf_sketch, merge_sketch):
    cols = columns - lax.axis_index("cell") * blocks.shape[0] + HB
    z, coeffs = merged_top(start_states, sources, blocks, cols, leaf_sketch, merge_sketch)
    return project(coeffs, z)


def solution(mesh):
    placed = (
        P("snap", "cell"),
        P(None, "snap", "cell"),
        P("cell", None, None),
        P("cell", None),
        P(),
        P(),
    )
    return jax.shard_map(
        local, mesh=mesh, in_specs=placed, out_specs=P("snap", "cell"), check_vma=False
    )
```

time: 1050 us -> 159 us (0.15)
  waiting for transfers between devices: 763 us -> 0 us
  other arithmetic: 167 us -> 0.01 us
  Pallas kernels: 0 us -> 154 us
  matrix products: 41 us -> 0 us
  local copies, waits for them, and re-layouts: 33.8 us -> 4.5 us
  between operations: 18.1 us -> 0.01 us
  starting transfers between devices: 17 us -> 0 us
    psum x4 -> x0, waiting for transfers between devices: 691 us -> none  [the longest x1 180 us: local(): leaf_total = lax.psum(gram_of(leaf_rows), 'cell')]
    pallas_call x0 -> x2, Pallas kernels: none -> 154 us  [the longest x1 151 us: merged_top(): pl.pallas_call(main_kernel, name='merged_top', out_shape=(jax.ShapeDtypeS...]
    another operation x37 -> x0, other arithmetic: 150 us -> none  [the longest x21 88.6 us: normalize(): lower = jnp.linalg.cholesky(gram)]
    ppermute x6 -> x0, waiting for transfers between devices: 71.4 us -> none  [the longest x2 68.4 us: swapped(): return lax.ppermute(value, axis, pairs)]
    dot_general x12 -> x0, matrix products: 32.4 us -> none  [the longest x3 6.52 us: gram_of(): return jnp.dot(z_rows, z_rows.T, precision=lax.Precision.HIGHEST)]
    gather x2 -> x0, local copies, waits for them, and re-layouts: 16.7 us -> none  [local(): jnp.take(padded, local_cols, axis=1).reshape(rows, nblocks, nstored * block)]
    ppermute x6 -> x0, starting transfers between devices: 16.1 us -> none  [the longest x2 8.11 us: with_halo(): lax.ppermute(lax.slice_in_dim(block, block.shape[dim] - width, None, axis...]
  transfers between devices with their start and end apart: 10 -> 0, of which waited for: 8 -> 0; matrix products, arithmetic and copies ran while one was open for 1% -> 0% of each run, Pallas kernels for 0% -> 0%
where the time goes in v2:
time: 159 us
  Pallas kernels  154 us (97%)
  local copies, waits for them, and re-layouts  4.5 us (3%)
    pallas_call x1, Pallas kernels, merged_top(): pl.pallas_call(main_kernel, name='merged_top', out_shape=(jax.ShapeDtypeS...  151 us
    unnamed x7, local copies, waits for them, and re-layouts  4.5 us

profile of v2, /device:TPU:1, one launch (start us, length us, event | category | flops | bytes accessed | tf_op | source)
XLA Modules:
  0.0 158.6 jit_solution(13239104277524803277)
XLA Ops:
  0.0 0.8 copy.8
  0.8 0.0 copy-start
  0.8 1.6 %copy-done = f32[256,2048]{1,0:T(8,128)S(1)} copy-done((f32[256,2048]{1,0:T(8,128)S(1)}, f32[256,2048]{1,0:T(8,128)}, u32[]{:S(2)}) %copy-start) | copy-done | bytes 2097176
  2.4 0.0 copy-start.1
  2.4 1.1 copy-done.1
  3.5 0.0 copy-start.2
  3.5 1.0 copy-done.2
  4.5 151.3 %merged_top.1 = (f32[4,200,512]{2,1,0:T(8,128)S(1)}, f32[256,200]{1,0:T(8,128)S(1)}) custom-call(f32[256,2048]{1,0:T(8,128)S(1)} %copy-done, bf16[2,256,2048]{2,1,0:T(8,128)(2,1)} %src_hbm.1, bf16[32,64,448]{2,1,0:T(8,128)(2,1)} %blk_hbm.1, s32[32,7]{1,0:T(8,128)S(1)} %subtract_add_fusion.cols_ref, f32[200,512]{1,0:T(8,128)S(1)} %copy-done.2, ...), custom_call_target="tpu_custom_call" | custom-call | tf_op jit(solution)/shard_map/merged_top/pallas_call | solution.py:405
  155.9 2.8 %project.1 = f32[256,2048]{1,0:T(8,128)} custom-call(f32[256,200]{1,0:T(8,128)S(1)} %get-tuple-element.7.co_ref, f32[4,200,512]{2,1,0:T(8,128)S(1)} %get-tuple-element.8.z_ref), custom_call_target="tpu_custom_call" | custom-call | tf_op jit(solution)/shard_map/project/pallas_call | solution.py:443
  (1 shorter events, 0.0 us)
Async XLA Ops:
  0.8 1.6 %copy-start = (f32[256,2048]{1,0:T(8,128)S(1)}, f32[256,2048]{1,0:T(8,128)}, u32[]{:S(2)}) copy-start(f32[256,2048]{1,0:T(8,128)} %x0_hbm.1) | copy-start | bytes 6291460
  2.4 1.1 copy-start.1
  3.5 1.0 copy-start.2

commit v3 on v2

v3 whole, which is shorter than its diff:
```python
import jax
import jax.numpy as jnp
from jax import lax
from jax.experimental import pallas as pl
from jax.experimental.pallas import tpu as pltpu
from jax.sharding import PartitionSpec as P

HB = 4
NZ = 8
NW = 8
NX = 4
NB = 40
MESH = pl.DeviceIdType.MESH
F32 = jnp.float32
BF16 = jnp.bfloat16


def mm(a, b):
    return jnp.dot(a, b, precision=lax.Precision.HIGHEST, preferred_element_type=F32)


def halves(a):
    high = a.astype(BF16)
    return high, (a - high.astype(F32)).astype(BF16)


def mm3(a, b):
    ah, al = halves(a)
    bh, bl = halves(b)
    small = jnp.dot(ah, bl, preferred_element_type=F32) + jnp.dot(al, bh, preferred_element_type=F32)
    return jnp.dot(ah, bh, preferred_element_type=F32) + small


def mm_nt(a, b):
    return lax.dot_general(
        a, b, (((1,), (1,)), ((), ())), precision=lax.Precision.HIGHEST, preferred_element_type=F32
    )


def eliminate(tiles):
    nt = len(tiles[0])
    sub = lax.broadcasted_iota(jnp.int32, (8, 128), 0)
    for t in range(nt):
        cols = [
            [
                [jnp.broadcast_to(r[u][:, 8 * t + j : 8 * t + j + 1], (8, 128)) for j in range(8)]
                for u in range(t, nt)
            ]
            for r in tiles
        ]
        for j in range(8):
            for r, cl in zip(tiles, cols):
                pivot = jnp.broadcast_to(cl[0][j][j : j + 1], (8, 128))
                inv = lax.rsqrt(pivot)
                row = jnp.broadcast_to(r[t][j : j + 1], (8, 128)) * inv
                heads = [jnp.broadcast_to(cl[0][j][m : m + 1], (8, 128)) * inv for m in range(j + 1, 8)]
                for u in range(t, nt):
                    lcol = cl[u - t][j] * inv
                    if u == t:
                        lcol = jnp.where(sub > j, lcol, 0.0)
                        r[u] = jnp.where(sub == j, row, r[u] - lcol * row)
                    else:
                        r[u] = r[u] - lcol * row
                    for m in range(j + 1, 8):
                        cl[u - t][m] = cl[u - t][m] - lcol * heads[m - j - 1]
    return tiles


def chol_inv(a_ref, batch, after=None):
    n = a_ref.shape[1]
    lane = lax.broadcasted_iota(jnp.int32, (NB, 128), 1)
    srow = lax.broadcasted_iota(jnp.int32, (NB, 128), 0)
    lane2 = lax.broadcasted_iota(jnp.int32, (NB, 256), 1)
    srow2 = lax.broadcasted_iota(jnp.int32, (NB, 256), 0)
    for k in range(n // NB):
        lo = k * NB
        hi = lo + NB
        tiles = []
        for b in range(batch):
            blk = a_ref[b, lo:hi, :]
            if lo:
                blk = pltpu.roll(blk, 256 - lo, axis=1)
            blk = jnp.where(lane < NB, blk[:, :128], jnp.where(lane == 64 + srow, 1.0, 0.0))
            tiles.append([blk[8 * t : 8 * t + 8] for t in range(NB // 8)])
        tiles = eliminate(tiles)
        for b in range(batch):
            tk = pltpu.roll(jnp.concatenate(tiles[b], axis=0), 64, axis=1)[:, :NB]
            own = jnp.where(lane2 - lo == srow2, 1.0, 0.0)
            w = mm(tk, jnp.where((lane2 >= lo) & (lane2 < hi), own, a_ref[b, lo:hi, :]))
            if hi < n:
                lane3 = lax.broadcasted_iota(jnp.int32, (n - hi, 256), 1)
                rest = jnp.where((lane3 >= lo) & (lane3 < hi), 0.0, a_ref[b, hi:, :])
                a_ref[b, hi:, :] = rest - mm(w.T[hi:n], w)
            a_ref[b, lo:hi, :] = jnp.where(lane2 < hi, w, 0.0)
        if after is not None:
            after(k)


def exchange(src_of, dst_of, count, me, device_of, send_sem, recv_sem):
    sends, waits = [], []
    for d in range(1, count):
        peer = lax.rem(me + d, count)
        origin = lax.rem(me + count - d, count)

        def copy(slot, peer=peer, d=d):
            return pltpu.make_async_remote_copy(
                src_ref=src_of(peer), dst_ref=dst_of(slot), send_sem=send_sem.at[d], recv_sem=recv_sem.at[slot],
                device_id=device_of(peer), device_id_type=MESH,
            )

        cp = copy(me)
        cp.start()
        sends.append(cp)
        waits.append(copy(origin))
    return sends, waits


def finish(pair):
    sends, waits = pair
    for w in waits:
        w.wait_recv()
    for s in sends:
        s.wait_send()


def add_up(ref, count):
    total = ref[0]
    for i in range(1, count):
        total = total + ref[i]
    return total


class Where:
    def __init__(self):
        self.x = lax.axis_index("snap")
        self.c = lax.axis_index("cell")
        self.z, self.w = self.c // NW, lax.rem(self.c, NW)

    def along_z(self, peer):
        return (self.x, peer * NW + self.w)

    def along_w(self, peer):
        return (self.x, self.z * NW + peer)

    def along_x(self, peer):
        return (peer, self.z * NW + self.w)


def reduce_steps(at, pk, size, bufs, over_snap):
    r1, r2, rx, out, ss, rs = bufs

    def piece(ref):
        return lambda i: ref.at[pl.ds(pl.multiple_of(i * size, 8), size)]

    def mine(ref):
        return lambda i: ref.at[i]

    here = pl.ds(pl.multiple_of(at.w * size, 8), size)
    going = exchange(piece(pk), mine(r1), NW, at.w, at.along_w, ss.at[0], rs.at[0])
    r1[at.w] = pk[here, :]
    yield
    finish(going)
    r2[at.z] = add_up(r1, NW)
    going = exchange(lambda _: r2.at[at.z], mine(r2), NZ, at.z, at.along_z, ss.at[1], rs.at[1])
    yield
    finish(going)
    total = add_up(r2, NZ)
    if over_snap:
        rx[at.x] = total
        going = exchange(lambda _: rx.at[at.x], mine(rx), NX, at.x, at.along_x, ss.at[2], rs.at[2])
        yield
        finish(going)
        total = add_up(rx, NX)
    out[here, :] = total
    going = exchange(lambda _: out.at[here], piece(out), NW, at.w, at.along_w, ss.at[3], rs.at[3])
    yield
    finish(going)


def run(steps):
    for _ in steps:
        pass


def pack(g, g_ref, pk, base):
    g_ref[:, : g.shape[1]] = g
    pk[base : base + 200, :] = g_ref[:, :128]
    pk[base + 200 : base + 272, :] = g_ref[128:200, 128:]


def unpack(pk, base, a_ref, b):
    a_ref[b, :, :128] = pk[base : base + 200, :]
    a_ref[b, 128:200, 128:] = pk[base + 200 : base + 272, :]
    a_ref[b, :128, 128:] = pk[base + 128 : base + 256, :].T


def main_kernel(
    x0_hbm, src_hbm, blk_hbm, cols_ref, sk_hbm, ms_hbm,
    zf_hbm, co_ref,
    zf_ref, x0_ref, src_ref, blk_ref, sk_ref, ms_ref, x1_ref, x2_ref, y_ref, dup_a, dup_b, out_h, in_h,
    yq, gs, u_ref, fac, tx, xr, ss_ref, d_ref,
    pk1, l1, l2, lo, pk2, p1, p2, px, po, pk3, c1, c2, co,
    in_sem, send_sem, recv_sem, s1, q1, s2, q2, s3, q3, sb, qb, st, qt,
):
    at = Where()
    x, c = at.x, at.c
    n = 200
    ncell = NZ * NW
    left, right = lax.rem(c + ncell - 1, ncell), lax.rem(c + 1, ncell)
    barrier = pltpu.get_barrier_semaphore()
    greeted = [(x, left), (x, right)]
    greeted += [at.along_z(lax.rem(at.z + d, NZ)) for d in range(1, NZ)]
    greeted += [at.along_w(lax.rem(at.w + d, NW)) for d in range(1, NW)]
    greeted += [at.along_x(lax.rem(at.x + d, NX)) for d in range(1, NX)]
    for device in greeted:
        pl.semaphore_signal(barrier, inc=1, device_id=device, device_id_type=MESH)
    moved = (
        (x0_hbm, x0_ref), (blk_hbm, blk_ref), (src_hbm.at[0], src_ref.at[0]), (src_hbm.at[1], src_ref.at[1]),
        (sk_hbm, sk_ref), (ms_hbm, ms_ref),
    )
    loads = [pltpu.make_async_copy(src, dst, in_sem.at[i]) for i, (src, dst) in enumerate(moved)]
    for ld in loads:
        ld.start()

    rows = x0_ref.shape[0]
    npair = x0_ref.shape[1] // 128
    low = lax.broadcasted_iota(jnp.int32, (rows, 128), 1) < 64

    def spread(tile, dup, p):
        turned = pltpu.roll(tile, 64, axis=1)
        dup[2 * p] = jnp.where(low, tile, turned).astype(BF16)
        dup[2 * p + 1] = jnp.where(low, turned, tile).astype(BF16)

    def lanes(p):
        return pl.ds(pl.multiple_of(p * 128, 128), 128)

    def copies(step):
        return [
            pltpu.make_async_remote_copy(
                src_ref=out_h.at[step, pl.ds(2 * side, 2)],
                dst_ref=in_h.at[step, pl.ds(2 - 2 * side, 2)],
                send_sem=send_sem.at[step, side],
                recv_sem=recv_sem.at[step, side],
                device_id=(x, peer),
                device_id_type=MESH,
            )
            for side, peer in ((0, left), (1, right))
        ]

    def apply(dup, xin, xout, s, p, then):
        sides = []
        for b2 in range(2):
            b = 2 * p + b2
            parts = []
            for jj in range(3):
                ca = cols_ref[2 * jj, b]
                cb = cols_ref[2 * jj + 1, b]
                parts.append(jnp.where(low, dup[ca], dup[cb]))
            parts.append(dup[cols_ref[6, b]][:, :64])
            picked = jnp.concatenate(parts, axis=1)
            sides.append(
                lax.dot_general(
                    picked, blk_ref[b], (((1,), (1,)), ((), ())), preferred_element_type=F32
                )
            )
        res = jnp.concatenate(sides, axis=1)
        new = xin[:, lanes(p)] - res + src_ref[s, :, lanes(p)].astype(F32)
        xout[:, lanes(p)] = new
        if then is not None:
            spread(new, then, p + 2)
        return new

    def arrive(step, dup):
        for e in range(2):
            spread(in_h[step, e].astype(F32), dup, e)
            spread(in_h[step, 2 + e].astype(F32), dup, npair + 2 + e)

    loads[0].wait()
    for e in range(2):
        out_h[0, e] = x0_ref[:, e * 128 : (e + 1) * 128].astype(BF16)
        q = npair - 2 + e
        out_h[0, 2 + e] = x0_ref[:, q * 128 : (q + 1) * 128].astype(BF16)
    pl.semaphore_wait(barrier, len(greeted))
    first = copies(0)
    for cp in first:
        cp.start()

    @pl.loop(0, npair)
    def _(p):
        spread(x0_ref[:, lanes(p)], dup_a, p + 2)

    loads[1].wait()
    loads[2].wait()

    @pl.loop(2, npair - 2)
    def _(p):
        apply(dup_a, x0_ref, x1_ref, 0, p, dup_b)

    for cp in first:
        cp.wait()
    arrive(0, dup_a)
    for e, p in enumerate((0, 1, npair - 2, npair - 1)):
        out_h[1, e] = apply(dup_a, x0_ref, x1_ref, 0, p, dup_b).astype(BF16)
    second = copies(1)
    for cp in second:
        cp.start()

    loads[3].wait()

    @pl.loop(2, npair - 2)
    def _(p):
        apply(dup_b, x1_ref, x2_ref, 1, p, None)

    for cp in second:
        cp.wait()
    arrive(1, dup_b)
    for p in (0, 1, npair - 2, npair - 1):
        apply(dup_b, x1_ref, x2_ref, 1, p, None)

    gs[...] = jnp.zeros_like(gs)
    loads[4].wait()
    gram = None
    for q in range(NX):
        cut = slice(q * 512, (q + 1) * 512)
        y_ref[q] = mm3(sk_ref[:, :rows], x1_ref[:, cut]) + mm3(sk_ref[:, rows:], x2_ref[:, cut])
        part = mm_nt(y_ref[q], y_ref[q])
        gram = part if gram is None else gram + part

    pk1[272:, :] = jnp.zeros((48, 128), F32)
    pack(gram, gs, pk1, 0)
    steps = reduce_steps(at, pk1, 40, (l1, l2, None, lo, s1, q1), False)
    next(steps)
    bulk = exchange(lambda peer: y_ref.at[peer], lambda i: yq.at[i], NX, x, at.along_x, sb.at[0], qb.at[0])
    yq[x] = y_ref[x]
    tx[:, :120, 128:] = jnp.zeros((NX, 120, 128), F32)
    pk2[888:, :] = jnp.zeros((8, 128), F32)
    pk3[...] = jnp.zeros_like(pk3)
    xr[...] = jnp.zeros_like(xr)
    d_ref[...] = jnp.zeros_like(d_ref)
    loads[5].wait()
    halves_of = [[ms_ref[level, :, n * h : n * h + n] for h in range(2)] for level in range(2)]
    ss_ref[...] = mm_nt(halves_of[1][0], halves_of[1][0]) + mm_nt(halves_of[1][1], halves_of[1][1])
    run(steps)
    unpack(lo, 0, fac, 0)
    shares = []

    def send_rows(k):
        part = (pl.ds(k * NB, NB), pl.ds(0, 128 if k < 3 else 256))
        shares.append(
            exchange(
                lambda _: fac.at[0, *part], lambda i: tx.at[i, *part], NX, x, at.along_x, st.at[k], qt.at[k]
            )
        )

    chol_inv(fac.at[pl.ds(0, 1)], 1, send_rows)
    tx[x] = fac[0]
    finish(bulk)
    for share in shares:
        finish(share)

    bulks = []
    for p in range(2):
        for h in range(2):
            u_ref[h, :, :n] = mm(halves_of[0][h], tx[2 * p + h][:, :n])
        m = mm(u_ref[0, :, :n], yq[2 * p]) + mm(u_ref[1, :, :n], yq[2 * p + 1])
        zf_ref[p, x] = m
        bulks.append(
            exchange(
                lambda _, p=p: zf_ref.at[p, x], lambda i, p=p: zf_ref.at[p, i],
                NX, x, at.along_x, sb.at[1 + p], qb.at[1 + p],
            )
        )
    for p in range(2):
        pack(mm_nt(zf_ref[p, x], zf_ref[p, x]), gs, pk2, 272 * p)
    pk2[544:744, :] = mm_nt(zf_ref[0, x], zf_ref[1, x, :128])
    xr[:, :n] = mm_nt(zf_ref[1, x, 128:], zf_ref[0, x])
    pk2[744:816, :] = xr[:, :128]
    pk2[816:888, :] = xr[:, 128:]
    steps = reduce_steps(at, pk2, 112, (p1, p2, px, po, s2, q2), True)
    next(steps)
    next(steps)
    for p in range(2):
        finish(bulks[p])
        raw = mm_nt(x2_ref[:, :512], zf_ref[p, 0])
        for q in range(1, NX):
            raw = raw + mm_nt(x2_ref[:, q * 512 : (q + 1) * 512], zf_ref[p, q])
        pk3[512 * p : 512 * p + 256, :] = raw[:, :128]
        pk3[512 * p + 256 : 512 * p + 512, :72] = raw[:, 128:]
        next(steps)
    keep = pltpu.make_async_copy(zf_ref, zf_hbm, in_sem.at[6])
    keep.start()
    last = reduce_steps(at, pk3, 128, (c1, c2, None, co, s3, q3), False)
    next(last)
    run(steps)

    for p in range(2):
        unpack(po, 272 * p, fac, p)
    gs[:, :128] = po[544:744, :]
    xr[:, :128] = po[744:816, :]
    xr[:, 128:] = po[816:888, :]
    gs[:, 128:n] = xr[...].T[:n]

    def go_on(k):
        if k == 1:
            next(last)

    chol_inv(fac, 2, go_on)
    for p in range(2):
        u_ref[p, :, :n] = mm(halves_of[1][p], fac[p][:, :n])
    d_ref[:, :n] = mm_nt(mm(u_ref[0, :, :n], gs[:, :n]), u_ref[1, :, :n])
    fac[0, :, :n] = ss_ref[...] + d_ref[:, :n] + d_ref[...].T[:n, :n]
    chol_inv(fac.at[pl.ds(0, 1)], 1, go_on)
    for p in range(2):
        u_ref[p, :, :n] = mm(fac[0][:, :n], u_ref[p, :, :n])
    run(last)
    inner = None
    for p in range(2):
        base = 512 * p
        part = mm_nt(co[base : base + 256, :], u_ref[p, :, :128])
        part = part + mm_nt(co[base + 256 : base + 512, :][:, :72], u_ref[p, :, 128:n])
        inner = part if inner is None else inner + part
    for p in range(2):
        co_ref[p] = mm(inner, u_ref[p, :, :n])
    keep.wait()


def merged_top(start_states, sources, blocks, cols, leaf_sketch, merge_sketch):
    rows, width = start_states.shape
    rank = leaf_sketch.shape[0]
    part = width // NX
    nblk = width // 64
    anywhere = pl.BlockSpec(memory_space=pl.ANY)
    vmem = pl.BlockSpec(memory_space=pltpu.VMEM)
    dma = pltpu.SemaphoreType.DMA

    def buf(*shape, dtype=F32):
        return pltpu.VMEM(shape, dtype)

    return pl.pallas_call(
        main_kernel,
        name="merged_top",
        out_shape=(
            jax.ShapeDtypeStruct((2, NX, rank, part), F32),
            jax.ShapeDtypeStruct((2, rows, rank), F32),
        ),
        in_specs=[anywhere] * 3 + [pl.BlockSpec(memory_space=pltpu.SMEM)] + [anywhere] * 2,
        out_specs=(anywhere, vmem),
        scratch_shapes=[
            buf(2, NX, rank, part), buf(rows, width), buf(*sources.shape, dtype=BF16), buf(*blocks.shape, dtype=BF16),
            buf(*leaf_sketch.shape), buf(*merge_sketch.shape),
            buf(rows, width), buf(rows, width), buf(NX, rank, part),
            buf(nblk + 2 * HB, rows, 128, dtype=BF16), buf(nblk + 2 * HB, rows, 128, dtype=BF16),
            buf(2, 4, rows, 128, dtype=BF16), buf(2, 4, rows, 128, dtype=BF16),
            buf(NX, rank, part), buf(rank, 256), buf(2, rank, 256), buf(2, rank, 256), buf(NX, rank, 256),
            buf(72, 256), buf(rank, rank), buf(rank, 256),
            buf(320, 128), buf(NW, 40, 128), buf(NZ, 40, 128), buf(320, 128),
            buf(896, 128), buf(NW, 112, 128), buf(NZ, 112, 128), buf(NX, 112, 128), buf(896, 128),
            buf(1024, 128), buf(NW, 128, 128), buf(NZ, 128, 128), buf(1024, 128),
            dma((7,)), dma((2, 2)), dma((2, 2)),
            dma((4, 8)), dma((4, 8)), dma((4, 8)), dma((4, 8)), dma((4, 8)), dma((4, 8)),
            dma((3, 4)), dma((3, 4)), dma((5, 4)), dma((5, 4)),
        ],
        compiler_params=pltpu.CompilerParams(
            collective_id=0, has_side_effects=True, vmem_limit_bytes=60 * 2**20
        ),
    )(start_states, sources, blocks, cols, leaf_sketch, merge_sketch)


def project_kernel(co_ref, z_ref, o_ref):
    o_ref[...] = mm3(co_ref[0], z_ref[0, 0]) + mm3(co_ref[1], z_ref[1, 0])


def project(coeffs, z):
    _, rows, rank = coeffs.shape
    parts, part = z.shape[1], z.shape[3]
    return pl.pallas_call(
        project_kernel,
        name="project",
        grid=(parts,),
        out_shape=jax.ShapeDtypeStruct((rows, parts * part), F32),
        in_specs=[
            pl.BlockSpec((2, rows, rank), lambda q: (0, 0, 0)),
            pl.BlockSpec((2, 1, rank, part), lambda q: (0, q, 0, 0)),
        ],
        out_specs=pl.BlockSpec((rows, part), lambda q: (0, q)),
        compiler_params=pltpu.CompilerParams(vmem_limit_bytes=60 * 2**20),
    )(coeffs, z)


def local(start_states, sources, blocks, columns, leaf_sketch, merge_sketch):
    cols = columns.T - lax.axis_index("cell") * blocks.shape[0] + HB
    z, coeffs = merged_top(start_states, sources, blocks, cols, leaf_sketch, merge_sketch)
    return project(coeffs, z)


def solution(mesh):
    placed = (
        P("snap", "cell"),
        P(None, "snap", "cell"),
        P("cell", None, None),
        P("cell", None),
        P(),
        P(),
    )
    return jax.shard_map(
        local, mesh=mesh, in_specs=placed, out_specs=P("snap", "cell"), check_vma=False
    )
```

time: 159 us -> 145 us (0.912)
  Pallas kernels: 154 us -> 144 us
  local copies, waits for them, and re-layouts: 4.5 us -> 0 us
    pallas_call x1, Pallas kernels: 151 us -> 138 us  [merged_top(): pl.pallas_call(main_kernel, name='merged_top', out_shape=(jax.ShapeDtypeS...]
    unnamed x7 -> x0, local copies, waits for them, and re-layouts: 4.5 us -> none
    pallas_call x1, Pallas kernels: 2.76 us -> 5.26 us  [project(): pl.pallas_call(project_kernel, name='project', grid=(parts,), out_shape=j...]
where the time goes in v3:
time: 145 us
  Pallas kernels  144 us (99%)
    pallas_call x1, Pallas kernels, merged_top(): pl.pallas_call(main_kernel, name='merged_top', out_shape=(jax.ShapeDtypeS...  138 us
    pallas_call x1, Pallas kernels, project(): pl.pallas_call(project_kernel, name='project', grid=(parts,), out_shape=j...  5.26 us

profile of v3, /device:TPU:1, one launch (start us, length us, event | category | flops | bytes accessed | tf_op | source)
XLA Modules:
  0.0 144.9 jit_solution(10901981388026158899)
XLA Ops:
  0.0 1.3 add_bitcast_fusion.cols_ref
  1.3 138.4 %merged_top.1 = (f32[2,4,200,512]{3,2,1,0:T(8,128)}, f32[2,256,200]{2,1,0:T(8,128)}) custom-call(f32[256,2048]{1,0:T(8,128)} %x0_hbm.1, bf16[2,256,2048]{2,1,0:T(8,128)(2,1)} %src_hbm.1, bf16[32,64,448]{2,1,0:T(8,128)(2,1)} %blk_hbm.1, s32[7,32]{1,0:T(8,128)} %add_bitcast_fusion.cols_ref, f32[200,512]{1,0:T(8,128)} %sk_hbm.1, f32[2,200,400]{2,1,0:T(8,128)} %ms_hbm.1), custom_call_target="tpu_custom_call" | custom-call | tf_op jit(solution)/shard_map/merged_top/pallas_call | solution.py:439
  139.7 5.3 %project.1 = f32[256,2048]{1,0:T(8,128)} custom-call(f32[2,256,200]{2,1,0:T(8,128)} %get-tuple-element.7.co_ref, f32[2,4,200,512]{3,2,1,0:T(8,128)} %get-tuple-element.8.z_ref), custom_call_target="tpu_custom_call" | custom-call | tf_op jit(solution)/shard_map/project/pallas_call | solution.py:476

commit v4 on v3

--- a/solution.py
+++ b/solution.py
@@ -199,8 +199,8 @@
     zf_hbm, co_ref,
     zf_ref, x0_ref, src_ref, blk_ref, sk_ref, ms_ref, x1_ref, x2_ref, y_ref, dup_a, dup_b, out_h, in_h,
     yq, gs, u_ref, fac, tx, xr, ss_ref, d_ref,
-    pk1, l1, l2, lo, pk2, p1, p2, px, po, pk3, c1, c2, co,
-    in_sem, send_sem, recv_sem, s1, q1, s2, q2, s3, q3, sb, qb, st, qt,
+    pk1, l1, l2, lo, pk2, p1, p2, px, po, pk3, c1, c2, co, pk4, e1, e2, eo,
+    in_sem, send_sem, recv_sem, s1, q1, s2, q2, s3, q3, s4, q4, sb, qb, st, qt,
 ):
     at = Where()
     x, c = at.x, at.c
@@ -335,6 +335,7 @@
     tx[:, :120, 128:] = jnp.zeros((NX, 120, 128), F32)
     pk2[888:, :] = jnp.zeros((8, 128), F32)
     pk3[...] = jnp.zeros_like(pk3)
+    pk4[...] = jnp.zeros_like(pk4)
     xr[...] = jnp.zeros_like(xr)
     d_ref[...] = jnp.zeros_like(d_ref)
     loads[5].wait()
@@ -358,40 +359,45 @@
     for share in shares:
         finish(share)
 
+    def send_pair(p, lo, hi, lane):
+        return exchange(
+            lambda _: zf_ref.at[p, x, lo:hi], lambda i: zf_ref.at[p, i, lo:hi],
+            NX, x, at.along_x, sb.at[lane], qb.at[lane],
+        )
+
+    def inner_products(p, pk):
+        raw = mm_nt(x2_ref[:, :512], zf_ref[p, 0])
+        for q in range(1, NX):
+            raw = raw + mm_nt(x2_ref[:, q * 512 : (q + 1) * 512], zf_ref[p, q])
+        pk[:rows, :] = raw[:, :128]
+        pk[rows:, :72] = raw[:, 128:]
+
     bulks = []
     for p in range(2):
         for h in range(2):
             u_ref[h, :, :n] = mm(halves_of[0][h], tx[2 * p + h][:, :n])
-        m = mm(u_ref[0, :, :n], yq[2 * p]) + mm(u_ref[1, :, :n], yq[2 * p + 1])
-        zf_ref[p, x] = m
-        bulks.append(
-            exchange(
-                lambda _, p=p: zf_ref.at[p, x], lambda i, p=p: zf_ref.at[p, i],
-                NX, x, at.along_x, sb.at[1 + p], qb.at[1 + p],
-            )
-        )
+        zf_ref[p, x] = mm(u_ref[0, :, :n], yq[2 * p]) + mm(u_ref[1, :, :n], yq[2 * p + 1])
+        bulks.append(send_pair(p, 0, (n, 56)[p], 1 + p))
     for p in range(2):
         pack(mm_nt(zf_ref[p, x], zf_ref[p, x]), gs, pk2, 272 * p)
     pk2[544:744, :] = mm_nt(zf_ref[0, x], zf_ref[1, x, :128])
     xr[:, :n] = mm_nt(zf_ref[1, x, 128:], zf_ref[0, x])
     pk2[744:816, :] = xr[:, :128]
     pk2[816:888, :] = xr[:, 128:]
-    steps = reduce_steps(at, pk2, 112, (p1, p2, px, po, s2, q2), True)
-    next(steps)
-    next(steps)
-    for p in range(2):
-        finish(bulks[p])
-        raw = mm_nt(x2_ref[:, :512], zf_ref[p, 0])
-        for q in range(1, NX):
-            raw = raw + mm_nt(x2_ref[:, q * 512 : (q + 1) * 512], zf_ref[p, q])
-        pk3[512 * p : 512 * p + 256, :] = raw[:, :128]
-        pk3[512 * p + 256 : 512 * p + 512, :72] = raw[:, 128:]
-        next(steps)
-    keep = pltpu.make_async_copy(zf_ref, zf_hbm, in_sem.at[6])
-    keep.start()
-    last = reduce_steps(at, pk3, 128, (c1, c2, None, co, s3, q3), False)
-    next(last)
-    run(steps)
+    products = reduce_steps(at, pk2, 112, (p1, p2, px, po, s2, q2), True)
+    first = reduce_steps(at, pk3, 64, (c1, c2, None, co, s3, q3), False)
+    second = reduce_steps(at, pk4, 64, (e1, e2, None, eo, s4, q4), False)
+    next(products)
+    next(products)
+    finish(bulks[0])
+    inner_products(0, pk3)
+    next(first)
+    next(products)
+    bulks.append(send_pair(1, 56, n, 3))
+    next(first)
+    next(products)
+    run(products)
+    next(first)
 
     for p in range(2):
         unpack(po, 272 * p, fac, p)
@@ -399,26 +405,38 @@
     xr[:, :128] = po[744:816, :]
     xr[:, 128:] = po[816:888, :]
     gs[:, 128:n] = xr[...].T[:n]
-
-    def go_on(k):
+    keep = pltpu.make_async_copy(zf_ref, zf_hbm, in_sem.at[6])
+
+    def during_pairs(k):
         if k == 1:
-            next(last)
-
-    chol_inv(fac, 2, go_on)
+            finish(bulks[1])
+            finish(bulks[2])
+            keep.start()
+            inner_products(1, pk4)
+            next(second)
+        if k == 4:
+            next(second)
+
+    def during_top(k):
+        if k == 2:
+            next(second)
+
+    chol_inv(fac, 2, during_pairs)
+    run(first)
     for p in range(2):
         u_ref[p, :, :n] = mm(halves_of[1][p], fac[p][:, :n])
     d_ref[:, :n] = mm_nt(mm(u_ref[0, :, :n], gs[:, :n]), u_ref[1, :, :n])
     fac[0, :, :n] = ss_ref[...] + d_ref[:, :n] + d_ref[...].T[:n, :n]
-    chol_inv(fac.at[pl.ds(0, 1)], 1, go_on)
+    chol_inv(fac.at[pl.ds(0, 1)], 1, during_top)
     for p in range(2):
         u_ref[p, :, :n] = mm(fac[0][:, :n], u_ref[p, :, :n])
-    run(last)
-    inner = None
-    for p in range(2):
-        base = 512 * p
-        part = mm_nt(co[base : base + 256, :], u_ref[p, :, :128])
-        part = part + mm_nt(co[base + 256 : base + 512, :][:, :72], u_ref[p, :, 128:n])
-        inner = part if inner is None else inner + part
+
+    def in_top(p, total):
+        return mm_nt(total[:rows, :], u_ref[p, :, :128]) + mm_nt(total[rows:, :][:, :72], u_ref[p, :, 128:n])
+
+    inner = in_top(0, co)
+    run(second)
+    inner = inner + in_top(1, eo)
     for p in range(2):
         co_ref[p] = mm(inner, u_ref[p, :, :n])
     keep.wait()
@@ -455,10 +473,11 @@
             buf(72, 256), buf(rank, rank), buf(rank, 256),
             buf(320, 128), buf(NW, 40, 128), buf(NZ, 40, 128), buf(320, 128),
             buf(896, 128), buf(NW, 112, 128), buf(NZ, 112, 128), buf(NX, 112, 128), buf(896, 128),
-            buf(1024, 128), buf(NW, 128, 128), buf(NZ, 128, 128), buf(1024, 128),
+            buf(512, 128), buf(NW, 64, 128), buf(NZ, 64, 128), buf(512, 128),
+            buf(512, 128), buf(NW, 64, 128), buf(NZ, 64, 128), buf(512, 128),
             dma((7,)), dma((2, 2)), dma((2, 2)),
-            dma((4, 8)), dma((4, 8)), dma((4, 8)), dma((4, 8)), dma((4, 8)), dma((4, 8)),
-            dma((3, 4)), dma((3, 4)), dma((5, 4)), dma((5, 4)),
+            dma((4, 8)), dma((4, 8)), dma((4, 8)), dma((4, 8)), dma((4, 8)), dma((4, 8)), dma((4, 8)), dma((4, 8)),
+            dma((4, 4)), dma((4, 4)), dma((5, 4)), dma((5, 4)),
         ],
         compiler_params=pltpu.CompilerParams(
             collective_id=0, has_side_effects=True, vmem_limit_bytes=60 * 2**20

time: 145 us -> 136 us (0.938)
  Pallas kernels: 144 us -> 134 us
    pallas_call x1, Pallas kernels: 138 us -> 128 us  [merged_top(): pl.pallas_call(main_kernel, name='merged_top', out_shape=(jax.ShapeDtypeS...]
where the time goes in v4:
time: 136 us; the launch traced here: 135 us
  Pallas kernels  134 us (99%)
    pallas_call x1, Pallas kernels, merged_top(): pl.pallas_call(main_kernel, name='merged_top', out_shape=(jax.ShapeDtypeS...  128 us
    pallas_call x1, Pallas kernels, project(): pl.pallas_call(project_kernel, name='project', grid=(parts,), out_shape=j...  5.26 us

profile of v4, /device:TPU:1, one launch (start us, length us, event | category | flops | bytes accessed | tf_op | source)
XLA Modules:
  0.0 135.0 jit_solution(15539394031032681456)
XLA Ops:
  0.0 1.3 add_bitcast_fusion.cols_ref
  1.3 128.5 %merged_top.1 = (f32[2,4,200,512]{3,2,1,0:T(8,128)}, f32[2,256,200]{2,1,0:T(8,128)}) custom-call(f32[256,2048]{1,0:T(8,128)} %x0_hbm.1, bf16[2,256,2048]{2,1,0:T(8,128)(2,1)} %src_hbm.1, bf16[32,64,448]{2,1,0:T(8,128)(2,1)} %blk_hbm.1, s32[7,32]{1,0:T(8,128)} %add_bitcast_fusion.cols_ref, f32[200,512]{1,0:T(8,128)} %sk_hbm.1, f32[2,200,400]{2,1,0:T(8,128)} %ms_hbm.1), custom_call_target="tpu_custom_call" | custom-call | tf_op jit(solution)/shard_map/merged_top/pallas_call | solution.py:457
  129.8 5.3 %project.1 = f32[256,2048]{1,0:T(8,128)} custom-call(f32[2,256,200]{2,1,0:T(8,128)} %get-tuple-element.7.co_ref, f32[2,4,200,512]{3,2,1,0:T(8,128)} %get-tuple-element.8.z_ref), custom_call_target="tpu_custom_call" | custom-call | tf_op jit(solution)/shard_map/project/pallas_call | solution.py:495

commit v5 on v4

--- a/solution.py
+++ b/solution.py
@@ -29,6 +29,15 @@
     bh, bl = halves(b)
     small = jnp.dot(ah, bl, preferred_element_type=F32) + jnp.dot(al, bh, preferred_element_type=F32)
     return jnp.dot(ah, bh, preferred_element_type=F32) + small
+
+
+def mm3_nt(a, b):
+    def dot(u, v):
+        return lax.dot_general(u, v, (((1,), (1,)), ((), ())), preferred_element_type=F32)
+
+    ah, al = halves(a)
+    bh, bl = halves(b)
+    return dot(ah, bh) + (dot(ah, bl) + dot(al, bh))
 
 
 def mm_nt(a, b):
@@ -199,8 +208,8 @@
     zf_hbm, co_ref,
     zf_ref, x0_ref, src_ref, blk_ref, sk_ref, ms_ref, x1_ref, x2_ref, y_ref, dup_a, dup_b, out_h, in_h,
     yq, gs, u_ref, fac, tx, xr, ss_ref, d_ref,
-    pk1, l1, l2, lo, pk2, p1, p2, px, po, pk3, c1, c2, co, pk4, e1, e2, eo,
-    in_sem, send_sem, recv_sem, s1, q1, s2, q2, s3, q3, s4, q4, sb, qb, st, qt,
+    pk1, l1, l2, lo, pk2, p1, p2, px, po, pk3, c1, c2, co, pk4, e1, e2, eo, pk5, r1, r2, rx, ro,
+    in_sem, send_sem, recv_sem, s1, q1, s2, q2, s3, q3, s4, q4, s5, q5, sb, qb, st, qt,
 ):
     at = Where()
     x, c = at.x, at.c
@@ -311,6 +320,9 @@
     def _(p):
         apply(dup_b, x1_ref, x2_ref, 1, p, None)
 
+    loads[4].wait()
+    for q in range(NX):
+        y_ref[q] = mm3(sk_ref[:, :rows], x1_ref[:, q * 512 : (q + 1) * 512])
     for cp in second:
         cp.wait()
     arrive(1, dup_b)
@@ -318,11 +330,10 @@
         apply(dup_b, x1_ref, x2_ref, 1, p, None)
 
     gs[...] = jnp.zeros_like(gs)
-    loads[4].wait()
     gram = None
     for q in range(NX):
         cut = slice(q * 512, (q + 1) * 512)
-        y_ref[q] = mm3(sk_ref[:, :rows], x1_ref[:, cut]) + mm3(sk_ref[:, rows:], x2_ref[:, cut])
+        y_ref[q] += mm3(sk_ref[:, rows:], x2_ref[:, cut])
         part = mm_nt(y_ref[q], y_ref[q])
         gram = part if gram is None else gram + part
 
@@ -333,7 +344,8 @@
     bulk = exchange(lambda peer: y_ref.at[peer], lambda i: yq.at[i], NX, x, at.along_x, sb.at[0], qb.at[0])
     yq[x] = y_ref[x]
     tx[:, :120, 128:] = jnp.zeros((NX, 120, 128), F32)
-    pk2[888:, :] = jnp.zeros((8, 128), F32)
+    pk2[544:, :] = jnp.zeros((32, 128), F32)
+    pk5[n + 144 :, :] = jnp.zeros((40, 128), F32)
     pk3[...] = jnp.zeros_like(pk3)
     pk4[...] = jnp.zeros_like(pk4)
     xr[...] = jnp.zeros_like(xr)
@@ -366,9 +378,9 @@
         )
 
     def inner_products(p, pk):
-        raw = mm_nt(x2_ref[:, :512], zf_ref[p, 0])
+        raw = mm3_nt(x2_ref[:, :512], zf_ref[p, 0])
         for q in range(1, NX):
-            raw = raw + mm_nt(x2_ref[:, q * 512 : (q + 1) * 512], zf_ref[p, q])
+            raw = raw + mm3_nt(x2_ref[:, q * 512 : (q + 1) * 512], zf_ref[p, q])
         pk[:rows, :] = raw[:, :128]
         pk[rows:, :72] = raw[:, 128:]
 
@@ -376,55 +388,64 @@
     for p in range(2):
         for h in range(2):
             u_ref[h, :, :n] = mm(halves_of[0][h], tx[2 * p + h][:, :n])
-        zf_ref[p, x] = mm(u_ref[0, :, :n], yq[2 * p]) + mm(u_ref[1, :, :n], yq[2 * p + 1])
-        bulks.append(send_pair(p, 0, (n, 56)[p], 1 + p))
+        zf_ref[p, x] = mm3(u_ref[0, :, :n], yq[2 * p]) + mm3(u_ref[1, :, :n], yq[2 * p + 1])
+        if p == 0:
+            bulks.append(send_pair(0, 0, n, 1))
     for p in range(2):
         pack(mm_nt(zf_ref[p, x], zf_ref[p, x]), gs, pk2, 272 * p)
-    pk2[544:744, :] = mm_nt(zf_ref[0, x], zf_ref[1, x, :128])
+    grams = reduce_steps(at, pk2, 72, (p1, p2, px, po, s2, q2), True)
+    next(grams)
+    pk5[:n, :] = mm_nt(zf_ref[0, x], zf_ref[1, x, :128])
     xr[:, :n] = mm_nt(zf_ref[1, x, 128:], zf_ref[0, x])
-    pk2[744:816, :] = xr[:, :128]
-    pk2[816:888, :] = xr[:, 128:]
-    products = reduce_steps(at, pk2, 112, (p1, p2, px, po, s2, q2), True)
+    pk5[n : n + 72, :] = xr[:, :128]
+    pk5[n + 72 : n + 144, :] = xr[:, 128:]
+    cross = reduce_steps(at, pk5, 48, (r1, r2, rx, ro, s5, q5), True)
     first = reduce_steps(at, pk3, 64, (c1, c2, None, co, s3, q3), False)
     second = reduce_steps(at, pk4, 64, (e1, e2, None, eo, s4, q4), False)
-    next(products)
-    next(products)
+    next(cross)
+    next(grams)
+    next(cross)
+    next(grams)
+    bulks.append(send_pair(1, 0, 80, 2))
     finish(bulks[0])
     inner_products(0, pk3)
     next(first)
-    next(products)
-    bulks.append(send_pair(1, 56, n, 3))
+    next(grams)
+    next(cross)
+    bulks.append(send_pair(1, 80, n, 3))
     next(first)
-    next(products)
-    run(products)
-    next(first)
+    run(grams)
 
     for p in range(2):
         unpack(po, 272 * p, fac, p)
-    gs[:, :128] = po[544:744, :]
-    xr[:, :128] = po[744:816, :]
-    xr[:, 128:] = po[816:888, :]
-    gs[:, 128:n] = xr[...].T[:n]
     keep = pltpu.make_async_copy(zf_ref, zf_hbm, in_sem.at[6])
 
     def during_pairs(k):
         if k == 1:
-            finish(bulks[1])
-            finish(bulks[2])
-            keep.start()
-            inner_products(1, pk4)
+            next(cross)
+        if k == 2:
+            next(first)
+
+    def during_top(k):
+        if k == 2:
             next(second)
         if k == 4:
             next(second)
 
-    def during_top(k):
-        if k == 2:
-            next(second)
-
     chol_inv(fac, 2, during_pairs)
-    run(first)
     for p in range(2):
         u_ref[p, :, :n] = mm(halves_of[1][p], fac[p][:, :n])
+    finish(bulks[1])
+    finish(bulks[2])
+    keep.start()
+    inner_products(1, pk4)
+    next(second)
+    run(first)
+    run(cross)
+    gs[:, :128] = ro[:n, :]
+    xr[:, :128] = ro[n : n + 72, :]
+    xr[:, 128:] = ro[n + 72 : n + 144, :]
+    gs[:, 128:n] = xr[...].T[:n]
     d_ref[:, :n] = mm_nt(mm(u_ref[0, :, :n], gs[:, :n]), u_ref[1, :, :n])
     fac[0, :, :n] = ss_ref[...] + d_ref[:, :n] + d_ref[...].T[:n, :n]
     chol_inv(fac.at[pl.ds(0, 1)], 1, during_top)
@@ -472,11 +493,12 @@
             buf(NX, rank, part), buf(rank, 256), buf(2, rank, 256), buf(2, rank, 256), buf(NX, rank, 256),
             buf(72, 256), buf(rank, rank), buf(rank, 256),
             buf(320, 128), buf(NW, 40, 128), buf(NZ, 40, 128), buf(320, 128),
-            buf(896, 128), buf(NW, 112, 128), buf(NZ, 112, 128), buf(NX, 112, 128), buf(896, 128),
+            buf(576, 128), buf(NW, 72, 128), buf(NZ, 72, 128), buf(NX, 72, 128), buf(576, 128),
             buf(512, 128), buf(NW, 64, 128), buf(NZ, 64, 128), buf(512, 128),
             buf(512, 128), buf(NW, 64, 128), buf(NZ, 64, 128), buf(512, 128),
+            buf(384, 128), buf(NW, 48, 128), buf(NZ, 48, 128), buf(NX, 48, 128), buf(384, 128),
             dma((7,)), dma((2, 2)), dma((2, 2)),
-            dma((4, 8)), dma((4, 8)), dma((4, 8)), dma((4, 8)), dma((4, 8)), dma((4, 8)), dma((4, 8)), dma((4, 8)),
+            dma((4, 8)), dma((4, 8)), dma((4, 8)), dma((4, 8)), dma((4, 8)), dma((4, 8)), dma((4, 8)), dma((4, 8)), dma((4, 8)), dma((4, 8)),
             dma((4, 4)), dma((4, 4)), dma((5, 4)), dma((5, 4)),
         ],
         compiler_params=pltpu.CompilerParams(

time: 136 us -> 132 us (0.971)
  Pallas kernels: 134 us -> 131 us
    pallas_call x1, Pallas kernels: 128 us -> 126 us  [merged_top(): pl.pallas_call(main_kernel, name='merged_top', out_shape=(jax.ShapeDtypeS...]
where the time goes in v5:
time: 132 us
  Pallas kernels  131 us (99%)
    pallas_call x1, Pallas kernels, merged_top(): pl.pallas_call(main_kernel, name='merged_top', out_shape=(jax.ShapeDtypeS...  126 us
    pallas_call x1, Pallas kernels, project(): pl.pallas_call(project_kernel, name='project', grid=(parts,), out_shape=j...  5.26 us

profile of v5, /device:TPU:1, one launch (start us, length us, event | category | flops | bytes accessed | tf_op | source)
XLA Modules:
  0.0 132.3 jit_solution(11062271262986450526)
XLA Ops:
  0.0 1.3 add_bitcast_fusion.cols_ref
  1.3 125.7 %merged_top.1 = (f32[2,4,200,512]{3,2,1,0:T(8,128)}, f32[2,256,200]{2,1,0:T(8,128)}) custom-call(f32[256,2048]{1,0:T(8,128)} %x0_hbm.1, bf16[2,256,2048]{2,1,0:T(8,128)(2,1)} %src_hbm.1, bf16[32,64,448]{2,1,0:T(8,128)(2,1)} %blk_hbm.1, s32[7,32]{1,0:T(8,128)} %add_bitcast_fusion.cols_ref, f32[200,512]{1,0:T(8,128)} %sk_hbm.1, f32[2,200,400]{2,1,0:T(8,128)} %ms_hbm.1), custom_call_target="tpu_custom_call" | custom-call | tf_op jit(solution)/shard_map/merged_top/pallas_call | solution.py:478
  127.0 5.3 %project.1 = f32[256,2048]{1,0:T(8,128)} custom-call(f32[2,256,200]{2,1,0:T(8,128)} %get-tuple-element.7.co_ref, f32[2,4,200,512]{3,2,1,0:T(8,128)} %get-tuple-element.8.z_ref), custom_call_target="tpu_custom_call" | custom-call | tf_op jit(solution)/shard_map/project/pallas_call | solution.py:517
